TPU v7x, 128 devices: a whole 4x4x4 slice. The times are simulated.
128 devices in a mesh: fsdp: 2 (over z_lo), ctx: 8 (over z_hi, y), tp: 8 (over x, core).
Axes of the slice: x: 4, y: 4, z: 4 (z_hi: 2, z_lo: 2; z = z_hi * 2 + z_lo), core: 2. Of those that a mesh axis runs over, the one named last changes fastest.
Arguments:
- tokens: bfloat16 [2, 3072, 2048], P('fsdp', 'ctx'), may hold values from -6 to 6
- norm_in: float32 [2048], replicated, may hold values from 0.5 to 1.5
- norm_mid: float32 [2048], replicated, may hold values from 0.5 to 1.5
- router_att: float32 [2048, 8], replicated, may hold values from -0.09375 to 0.09375
- router_mlp: float32 [2048, 8], replicated, may hold values from -0.09375 to 0.09375
- kv_weight: bfloat16 [2, 2048, 2048], P(None, ('fsdp', 'ctx'), 'tp'), may hold values from -0.1875 to 0.1875
- query_weight: bfloat16 [8, 2048, 2048], P('ctx', 'fsdp', 'tp'), may hold values from -0.1875 to 0.1875
- output_weight: bfloat16 [8, 2048, 2048], P('ctx', 'tp', 'fsdp'), may hold values from -0.5 to 0.5
- gate_up_weight: bfloat16 [8, 2, 2048, 5632], P('ctx', None, 'fsdp', 'tp'), may hold values from -0.125 to 0.125
- down_weight: bfloat16 [8, 5632, 2048], P('ctx', 'tp', 'fsdp'), may hold values from -0.109375 to 0.109375
- routes_att: int32 [2, 3072, 2], P('fsdp', 'ctx'), may hold values from 0 to 7, all different within a row
- routes_mlp: int32 [2, 3072, 2], P('fsdp', 'ctx'), may hold values from 0 to 7, all different within a row
- cotangent: bfloat16 [2, 3072, 2048], P('fsdp', 'ctx'), may hold values from -6 to 6
Outputs:
- output: bfloat16 [2, 3072, 2048], P('fsdp', 'ctx')
- input_grad: float32 [2, 3072, 2048], P('fsdp', 'ctx')
- norm_in_grad: float32 [2048], P(('fsdp', 'ctx'))
- norm_mid_grad: float32 [2048], P(('fsdp', 'ctx'))
- router_att_grad: float32 [2048, 8], P(('fsdp', 'ctx'))
- router_mlp_grad: float32 [2048, 8], P(('fsdp', 'ctx'))
- kv_weight_grad: float32 [2, 2048, 2048], P(None, ('fsdp', 'ctx'), 'tp')
- query_weight_grad: float32 [8, 2048, 2048], P('ctx', 'fsdp', 'tp')
- output_weight_grad: float32 [8, 2048, 2048], P('ctx', 'tp', 'fsdp')
- gate_up_weight_grad: float32 [8, 2, 2048, 5632], P('ctx', None, 'fsdp', 'tp')
- down_weight_grad: float32 [8, 5632, 2048], P('ctx', 'tp', 'fsdp')
Inputs may be any that keep to these rules, and one draw needn't show every extreme that they name: `routes_att`: each position names two different experts. `routes_mlp`: each position names two different experts.
All inputs are finite; a program needn't handle non-finite values.
Results may differ from a plain program's by a relative error of at most 0.025.
Values may be sent and summed in bfloat16 or wider, within the bound.
A program may use at most 256 MiB of HBM per device.

v0:
```python
from functools import partial

import jax
import jax.numpy as jnp
from jax import lax
from jax.sharding import PartitionSpec as P

HD = 128


epsilon = 1e-06
masked_score = -1e30
query_rows_most = 1024


def route_slots(routes_block, experts, capacity):
    count_rows, chosen = routes_block.shape
    flattened = routes_block.reshape(-1)
    labels = jnp.arange(experts, dtype=jnp.int32)
    onehot = (flattened[:, None] == labels[None, :]).astype(jnp.int32)
    before = jnp.cumsum(onehot, axis=0, dtype=jnp.int32) - onehot
    placed = jnp.sum(before * onehot, axis=1, dtype=jnp.int32)
    retained = placed < capacity
    dumped = experts * capacity
    target = jnp.where(retained, flattened * capacity + placed, dumped)
    source = jnp.arange(count_rows * chosen, dtype=jnp.int32) // chosen
    slot_token = jnp.zeros((dumped,), jnp.int32).at[target].set(source, mode="drop")
    filled = jnp.zeros((dumped,), jnp.float32).at[target].set(1.0, mode="drop")
    return (
        target.reshape(count_rows, chosen),
        retained.reshape(count_rows, chosen),
        slot_token,
        filled,
    )


def norm_forward(values, gain_vector):
    row_scale = lax.rsqrt(jnp.mean(values * values, axis=1, keepdims=True) + epsilon)
    return (values * row_scale * gain_vector, row_scale)


def norm_backward(values, row_scale, gain_vector, grad_normed):
    gain_grad = jnp.sum(grad_normed * values * row_scale, axis=0)
    scaled = grad_normed * gain_vector
    inner_sum = jnp.sum(scaled * values, axis=1, keepdims=True)
    return (row_scale * scaled - values * row_scale**3 * inner_sum / values.shape[1], gain_grad)


def chosen_gates(logits, routes):
    picked = jnp.take_along_axis(logits, routes, axis=1)
    return jax.nn.softmax(picked, axis=1)


def gates_backward(gates, grad_gates, routes, experts):
    inner_sum = jnp.sum(gates * grad_gates, axis=1, keepdims=True)
    grad_picked = gates * (grad_gates - inner_sum)
    labels = jnp.arange(experts, dtype=jnp.int32)
    matches = (routes[:, :, None] == labels[None, None, :]).astype(jnp.float32)
    return jnp.sum(grad_picked[:, :, None] * matches, axis=1)


def combine_rows(returned, target, weight):
    clipped = jnp.minimum(target, returned.shape[0] - 1)
    picked = jnp.take(returned, clipped.reshape(-1), axis=0).astype(jnp.float32)
    picked = picked.reshape(target.shape[0], target.shape[1], -1)
    return (jnp.sum(picked * weight[:, :, None], axis=1), picked)


def local(
    tokens,
    norm_in,
    norm_mid,
    router_att,
    router_mlp,
    kv_weight,
    query_weight,
    output_weight,
    gate_up_weight,
    down_weight,
    routes_att,
    routes_mlp,
    cotangent,
):
    experts = lax.axis_size("ctx")
    block_at = lax.axis_index("ctx")
    inputs = tokens[0].astype(jnp.float32)
    count_rows, model_width = inputs.shape
    chosen = routes_att.shape[2]
    capacity = count_rows * chosen // experts
    slot_count = experts * capacity
    local_width = query_weight.shape[2]
    heads_here = local_width // HD
    score_scale = HD ** (-0.5)
    block_rows = min(slot_count, query_rows_most)
    block_count = slot_count // block_rows
    kv_full = lax.all_gather(kv_weight, ("fsdp", "ctx"), axis=1, tiled=True)
    query_full, output_full, gate_up_full, down_full = (
        lax.all_gather(query_weight[0], "fsdp", axis=0, tiled=True),
        lax.all_gather(output_weight[0], "fsdp", axis=1, tiled=True),
        lax.all_gather(gate_up_weight[0], "fsdp", axis=1, tiled=True),
        lax.all_gather(down_weight[0], "fsdp", axis=1, tiled=True),
    )
    route_pair = jnp.concatenate([routes_att[0], routes_mlp[0]], axis=1)
    route_all = lax.all_gather(route_pair, "ctx", axis=0, tiled=True)
    route_blocks = route_all.reshape(experts, count_rows, 2 * chosen)

    def tables(route_part):
        target, retained, slot_token, filled = jax.vmap(
            partial(route_slots, experts=experts, capacity=capacity)
        )(route_part)
        owned_tokens = lax.dynamic_index_in_dim(
            slot_token.reshape(experts, experts, capacity), block_at, 1, keepdims=False
        )
        offsets = jnp.arange(experts, dtype=jnp.int32)[:, None] * count_rows
        positions = (owned_tokens + offsets).reshape(-1)
        home_tables = [
            lax.dynamic_index_in_dim(entries, block_at, 0, keepdims=False)
            for entries in (target, retained, slot_token, filled)
        ]
        return (
            home_tables[0],
            home_tables[1].astype(jnp.float32),
            home_tables[2],
            home_tables[3],
            positions,
        )

    att_target, att_retained, att_slot_token, att_filled, att_positions = tables(
        route_blocks[:, :, :chosen]
    )
    mlp_target, mlp_retained, mlp_slot_token, mlp_filled, mlp_positions = tables(
        route_blocks[:, :, chosen:]
    )

    def dispatch(lowered_rows, slot_token, filled):
        picked = jnp.take(lowered_rows, slot_token, axis=0)
        picked = jnp.where(filled[:, None] > 0, picked, jnp.zeros_like(picked))
        return picked.reshape(experts, capacity, model_width)

    def to_experts(home_rows):
        arrived = lax.all_to_all(home_rows, "ctx", split_axis=0, concat_axis=0, tiled=True)
        return arrived.reshape(slot_count, model_width)

    def to_home(partial_rows):
        partial_rows = partial_rows.reshape(experts, capacity, model_width)
        summed = lax.psum(partial_rows, "tp")
        returned = lax.all_to_all(
            summed.astype(jnp.bfloat16), "ctx", split_axis=0, concat_axis=0, tiled=True
        )
        return returned.reshape(slot_count, model_width)

    def slot_grads(grad_rows, target, weight, slot_token):
        slot_weight = (
            jnp.zeros((slot_count,), jnp.float32)
            .at[target.reshape(-1)]
            .set(weight.reshape(-1), mode="drop")
        )
        picked = jnp.take(grad_rows, slot_token, axis=0) * slot_weight[:, None]
        return picked.astype(jnp.bfloat16).reshape(experts, capacity, model_width)

    def undispatch(grad_slots, target, retained):
        summed, picked = combine_rows(grad_slots, target, retained)
        return summed

    normed, scale_in = norm_forward(inputs, norm_in)
    lowered = normed.astype(jnp.bfloat16)
    lowered_wide = lowered.astype(jnp.float32)
    gates_att = chosen_gates(
        jnp.dot(lowered_wide, router_att, precision=lax.Precision.HIGHEST), routes_att[0]
    )
    kv_local = jnp.einsum(
        "td,jdf->tjf", lowered, kv_full, preferred_element_type=jnp.float32
    ).astype(jnp.bfloat16)
    kv_sequence = lax.all_gather(
        kv_local.reshape(count_rows, 2 * local_width), "ctx", axis=0, tiled=True
    )
    length = kv_sequence.shape[0]
    keys_heads = kv_sequence[:, :local_width].reshape(length, heads_here, HD)
    values_heads = kv_sequence[:, local_width:].reshape(length, heads_here, HD)
    key_positions = jnp.arange(length, dtype=jnp.int32)
    rows_att = to_experts(dispatch(lowered, att_slot_token, att_filled))
    queries = jnp.dot(rows_att, query_full, preferred_element_type=jnp.float32).astype(jnp.bfloat16)
    queries_blocks = queries.reshape(block_count, block_rows, heads_here, HD)
    positions_blocks = att_positions.reshape(block_count, block_rows)

    def score_block(query_block, position_block):
        scores = (
            jnp.einsum("rhk,shk->hrs", query_block, keys_heads, preferred_element_type=jnp.float32)
            * score_scale
        )
        allowed = key_positions[None, None, :] <= position_block[None, :, None]
        return jnp.where(allowed, scores, masked_score)

    def attend_forward(packed):
        query_block, position_block = packed
        scores = score_block(query_block, position_block)
        highest = jnp.max(scores, axis=2, keepdims=True)
        raised = jnp.exp(scores - highest)
        totals = jnp.sum(raised, axis=2, keepdims=True)
        weights_soft = raised / totals
        mixed_values = jnp.einsum(
            "hrs,shk->rhk",
            weights_soft.astype(jnp.bfloat16),
            values_heads,
            preferred_element_type=jnp.float32,
        )
        return (mixed_values.astype(jnp.bfloat16), (highest + jnp.log(totals))[:, :, 0])

    attended, log_totals = lax.map(attend_forward, (queries_blocks, positions_blocks))
    attended = attended.reshape(slot_count, local_width)
    projected = to_home(jnp.dot(attended, output_full, preferred_element_type=jnp.float32))
    att_weight = gates_att * att_retained
    branch_att, att_picked = combine_rows(projected, att_target, att_weight)
    hidden = inputs + branch_att
    normed_mid, scale_mid = norm_forward(hidden, norm_mid)
    lowered_mid = normed_mid.astype(jnp.bfloat16)
    lowered_mid_wide = lowered_mid.astype(jnp.float32)
    gates_mlp = chosen_gates(
        jnp.dot(lowered_mid_wide, router_mlp, precision=lax.Precision.HIGHEST), routes_mlp[0]
    )
    rows_mlp = to_experts(dispatch(lowered_mid, mlp_slot_token, mlp_filled))
    gate_up = jnp.einsum("rd,jdf->jrf", rows_mlp, gate_up_full, preferred_element_type=jnp.float32)
    gate_pre = gate_up[0]
    up_value = gate_up[1]
    sigmoid_gate = jax.nn.sigmoid(gate_pre)
    silu_gate = gate_pre * sigmoid_gate
    hidden_units = (silu_gate * up_value).astype(jnp.bfloat16)
    mlp_out = to_home(jnp.dot(hidden_units, down_full, preferred_element_type=jnp.float32))
    mlp_weight = gates_mlp * mlp_retained
    branch_mlp, mlp_picked = combine_rows(mlp_out, mlp_target, mlp_weight)
    result = (hidden + branch_mlp).astype(jnp.bfloat16)
    grad_out = cotangent[0].astype(jnp.float32)
    grad_gates_mlp = jnp.sum(mlp_picked * grad_out[:, None, :], axis=2) * mlp_retained
    grad_logits_mlp = gates_backward(gates_mlp, grad_gates_mlp, routes_mlp[0], experts)
    router_mlp_grad = jnp.dot(lowered_mid_wide.T, grad_logits_mlp, precision=lax.Precision.HIGHEST)
    grad_lowered_mid = jnp.dot(grad_logits_mlp, router_mlp.T, precision=lax.Precision.HIGHEST)
    grad_mlp_slots = to_experts(slot_grads(grad_out, mlp_target, mlp_weight, mlp_slot_token))
    grad_units = jnp.dot(grad_mlp_slots, down_full.T, preferred_element_type=jnp.float32)
    down_grad = jnp.dot(hidden_units.T, grad_mlp_slots, preferred_element_type=jnp.float32)
    silu_slope = sigmoid_gate * (1.0 + gate_pre * (1.0 - sigmoid_gate))
    grad_gate = (grad_units * up_value * silu_slope).astype(jnp.bfloat16)
    grad_up = (grad_units * silu_gate).astype(jnp.bfloat16)
    grad_gate_up = jnp.stack([grad_gate, grad_up])
    gate_up_grad = jnp.einsum(
        "rd,jrf->jdf", rows_mlp, grad_gate_up, preferred_element_type=jnp.float32
    )
    grad_rows_mlp = to_home(
        jnp.einsum("jrf,jdf->rd", grad_gate_up, gate_up_full, preferred_element_type=jnp.float32)
    )
    grad_lowered_mid = grad_lowered_mid + undispatch(grad_rows_mlp, mlp_target, mlp_retained)
    grad_hidden_mid, norm_mid_grad = norm_backward(hidden, scale_mid, norm_mid, grad_lowered_mid)
    grad_hidden = grad_out + grad_hidden_mid
    grad_gates_att = jnp.sum(att_picked * grad_hidden[:, None, :], axis=2) * att_retained
    grad_logits_att = gates_backward(gates_att, grad_gates_att, routes_att[0], experts)
    router_att_grad = jnp.dot(lowered_wide.T, grad_logits_att, precision=lax.Precision.HIGHEST)
    grad_lowered = jnp.dot(grad_logits_att, router_att.T, precision=lax.Precision.HIGHEST)
    grad_projected = to_experts(slot_grads(grad_hidden, att_target, att_weight, att_slot_token))
    grad_attended = jnp.dot(
        grad_projected, output_full.T, preferred_element_type=jnp.float32
    ).astype(jnp.bfloat16)
    output_grad = jnp.dot(attended.T, grad_projected, preferred_element_type=jnp.float32)
    grad_blocks = grad_attended.reshape(block_count, block_rows, heads_here, HD)

    def attend_backward(carried, packed):
        keys_grad, values_grad = carried
        query_block, position_block, grad_block, log_total = packed
        scores = score_block(query_block, position_block)
        weights_soft = jnp.exp(scores - log_total[:, :, None])
        weights_low = weights_soft.astype(jnp.bfloat16)
        grad_weights = jnp.einsum(
            "rhk,shk->hrs", grad_block, values_heads, preferred_element_type=jnp.float32
        )
        inner_sum = jnp.sum(weights_soft * grad_weights, axis=2, keepdims=True)
        grad_scores = (weights_soft * (grad_weights - inner_sum)).astype(jnp.bfloat16)
        grad_query = (
            jnp.einsum("hrs,shk->rhk", grad_scores, keys_heads, preferred_element_type=jnp.float32)
            * score_scale
        )
        keys_grad = (
            keys_grad
            + jnp.einsum(
                "hrs,rhk->shk", grad_scores, query_block, preferred_element_type=jnp.float32
            )
            * score_scale
        )
        values_grad = values_grad + jnp.einsum(
            "hrs,rhk->shk", weights_low, grad_block, preferred_element_type=jnp.float32
        )
        return ((keys_grad, values_grad), grad_query.astype(jnp.bfloat16))

    zero_grads = jnp.zeros((length, heads_here, HD), jnp.float32)
    (keys_grad, values_grad), grad_queries = lax.scan(
        attend_backward,
        (zero_grads, zero_grads),
        (queries_blocks, positions_blocks, grad_blocks, log_totals),
    )
    grad_queries = grad_queries.reshape(slot_count, local_width)
    query_grad = jnp.dot(rows_att.T, grad_queries, preferred_element_type=jnp.float32)
    grad_rows_att = to_home(jnp.dot(grad_queries, query_full.T, preferred_element_type=jnp.float32))
    grad_lowered = grad_lowered + undispatch(grad_rows_att, att_target, att_retained)
    kv_grad_sequence = jnp.concatenate(
        [keys_grad.reshape(length, local_width), values_grad.reshape(length, local_width)], axis=1
    )
    kv_grad_block = lax.psum_scatter(
        kv_grad_sequence.astype(jnp.bfloat16), "ctx", scatter_dimension=0, tiled=True
    )
    kv_grad_low = kv_grad_block.reshape(count_rows, 2, local_width)
    kv_weight_grad = jnp.einsum(
        "td,tjf->jdf", lowered, kv_grad_low, preferred_element_type=jnp.float32
    )
    grad_lowered_kv = jnp.einsum(
        "tjf,jdf->td", kv_grad_low, kv_full, preferred_element_type=jnp.float32
    )
    grad_lowered = grad_lowered + lax.psum(grad_lowered_kv.astype(jnp.bfloat16), "tp").astype(
        jnp.float32
    )
    grad_inputs_norm, norm_in_grad = norm_backward(inputs, scale_in, norm_in, grad_lowered)
    input_grad = grad_hidden + grad_inputs_norm
    query_share, output_share, gate_up_share, down_share = (
        lax.psum_scatter(
            query_grad.astype(jnp.bfloat16), "fsdp", scatter_dimension=0, tiled=True
        ).astype(jnp.float32),
        lax.psum_scatter(
            output_grad.astype(jnp.bfloat16), "fsdp", scatter_dimension=1, tiled=True
        ).astype(jnp.float32),
        lax.psum_scatter(
            gate_up_grad.astype(jnp.bfloat16), "fsdp", scatter_dimension=1, tiled=True
        ).astype(jnp.float32),
        lax.psum_scatter(
            down_grad.astype(jnp.bfloat16), "fsdp", scatter_dimension=1, tiled=True
        ).astype(jnp.float32),
    )
    kv_share, norm_in_share, norm_mid_share, router_att_share, router_mlp_share = (
        lax.psum_scatter(
            kv_weight_grad.astype(jnp.bfloat16), ("fsdp", "ctx"), scatter_dimension=1, tiled=True
        ).astype(jnp.float32),
        lax.psum_scatter(
            norm_in_grad.astype(jnp.bfloat16), ("fsdp", "ctx"), scatter_dimension=0, tiled=True
        ).astype(jnp.float32),
        lax.psum_scatter(
            norm_mid_grad.astype(jnp.bfloat16), ("fsdp", "ctx"), scatter_dimension=0, tiled=True
        ).astype(jnp.float32),
        lax.psum_scatter(
            router_att_grad.astype(jnp.bfloat16), ("fsdp", "ctx"), scatter_dimension=0, tiled=True
        ).astype(jnp.float32),
        lax.psum_scatter(
            router_mlp_grad.astype(jnp.bfloat16), ("fsdp", "ctx"), scatter_dimension=0, tiled=True
        ).astype(jnp.float32),
    )
    return (
        result[None],
        input_grad[None],
        norm_in_share,
        norm_mid_share,
        router_att_share,
        router_mlp_share,
        kv_share,
        query_share[None],
        output_share[None],
        gate_up_share[None],
        down_share[None],
    )


def solution(mesh):
    placed = (
        P("fsdp", "ctx", None),
        P(),
        P(),
        P(),
        P(),
        P(None, ("fsdp", "ctx"), "tp"),
        P("ctx", "fsdp", "tp"),
        P("ctx", "tp", "fsdp"),
        P("ctx", None, "fsdp", "tp"),
        P("ctx", "tp", "fsdp"),
        P("fsdp", "ctx", None),
        P("fsdp", "ctx", None),
        P("fsdp", "ctx", None),
    )
    return jax.shard_map(
        local,
        mesh=mesh,
        in_specs=placed,
        out_specs=(
            P("fsdp", "ctx", None),
            P("fsdp", "ctx", None),
            P(("fsdp", "ctx")),
            P(("fsdp", "ctx")),
            P(("fsdp", "ctx"), None),
            P(("fsdp", "ctx"), None),
            P(None, ("fsdp", "ctx"), "tp"),
            P("ctx", "fsdp", "tp"),
            P("ctx", "tp", "fsdp"),
            P("ctx", None, "fsdp", "tp"),
            P("ctx", "tp", "fsdp"),
        ),
        check_vma=False,
    )
```

profile of v0, /device:TPU:1, one launch (start us, length us, event | category | flops | bytes accessed | tf_op | source)
XLA Modules:
  0.0 1630.6 jit_solution(3596367813851059297)
XLA Ops:
  14.0 61.9 %all-gather.11.cloned.1.call-done = bf16[2,2048,256]{1,2,0:T(8,128)(2,1)} async-done(((bf16[2,128,256]{1,2,0:T(8,128)(2,1)}), bf16[2,2048,256]{1,2,0:T(8,128)(2,1)}) %all-gather.11.cloned.1.call-update) | async-done | bytes 2097168 | tf_op jit(solution)/shard_map/all_gather | solution.py:96
  80.2 28.0 %all_gather.23 = s32[3072,4]{0,1:T(4,128)S(1)} all-gather(s32[384,4]{0,1:T(4,128)S(1)} %pad_add_fusion.2), channel_id=1, replica_groups=mesh['fsdp'=2,'ctx'=8,'tp'=8] {'ctx'}, dimensions={0}, use_global_device_ids=true | all-gather | bytes 55296 | tf_op jit(solution)/shard_map/all_gather | solution.py:104
  112.7 23.4 %reduce-window.14 = s32[8,8,6,128]{3,1,2,0:T(8,128)S(1)} reduce-window(s32[8,8,6,128]{3,1,2,0:T(8,128)} %fusion.79, s32[]{:T(128)} %constant.167.clone.1), window={size=1x1x1x128 pad=0_0x0_0x0_0x127_0}, to_apply=%region_1.2 | reduce-window | flops 6242304 | bytes 393220 | tf_op jit(solution)/shard_map/reduce-window
  144.1 25.8 %reduce-window.16 = s32[8,8,6,128]{3,1,2,0:T(8,128)} reduce-window(s32[8,8,6,128]{3,1,2,0:T(8,128)} %fusion.80, s32[]{:T(128)} %constant.167.clone.1), window={size=1x1x1x128 pad=0_0x0_0x0_0x127_0}, to_apply=%region_12.16 | reduce-window | flops 6242304 | bytes 393220 | tf_op jit(solution)/shard_map/reduce-window.2
  186.7 23.2 %scatter_custom_fusion.2 = s32[6144]{0:T(1024)S(1)} fusion(s32[6144]{0:T(1024)S(1)} %reshape.652, s32[6144]{0:T(1024)} %reshape.654, s32[]{:T(128)} %constant.167.clone.1), kind=kCustom, calls=%fused_computation.183 | custom fusion | bytes 25088
  210.5 23.0 %scatter_custom_fusion.3 = f32[6144]{0:T(1024)S(1)} fusion(s32[6144]{0:T(1024)S(1)} %reshape.652, f32[6144]{0:T(1024)S(1)} %broadcast.422, f32[]{:T(128)} %constant.164.clone.1), kind=kCustom, calls=%fused_computation.179 | custom fusion | bytes 24580
  256.8 13.3 all-to-all-done
  314.1 91.3 %all-reduce.10 = bf16[8,96,2048]{2,1,0:T(8,128)(2,1)} all-reduce(f32[8,96,2048]{2,1,0:T(8,128)} %fusion.71), channel_id=1, replica_groups=mesh['fsdp'=2,'ctx'=8,'tp'=8] {'tp'}, use_global_device_ids=true, to_apply=%region_8.10 | all-reduce | flops 1572864 | bytes 9437184 | tf_op jit(solution)/shard_map/psum | solution.py:146
  416.7 23.8 %scatter_custom_fusion.5 = s32[6144]{0:T(1024)} fusion(s32[6144]{0:T(1024)S(1)} %reshape.664, s32[6144]{0:T(1024)} %reshape.654, s32[]{:T(128)} %constant.167.clone.1), kind=kCustom, calls=%fused_computation.181 | custom fusion | bytes 25088
  440.4 23.7 %scatter_custom_fusion.4 = f32[6144]{0:T(1024)} fusion(s32[6144]{0:T(1024)S(1)} %reshape.664, f32[6144]{0:T(1024)} %copy-done.53, f32[]{:T(128)} %constant.164.clone.1), kind=kCustom, calls=%fused_computation.177 | custom fusion | bytes 25088
  497.4 10.4 multiply_reduce_fusion.6
  549.0 15.4 all-to-all-done.2
  589.0 37.0 %all-gather.21.cloned.1.call-done = bf16[1,704,2048]{2,1,0:T(8,128)(2,1)} async-done(((bf16[1,704,1024]{2,1,0:T(8,128)(2,1)}), bf16[1,704,2048]{2,1,0:T(8,128)(2,1)}) %all-gather.21.cloned.1.call-update) | async-done | bytes 2883600 | tf_op jit(solution)/shard_map/all_gather | solution.py:101
  633.1 10.4 fusion.8
  655.1 132.6 %all-reduce.11 = (bf16[8,96,2048]{2,1,0:T(8,128)(2,1)}, bf16[8,96,2048]{2,1,0:T(8,128)(2,1)}) all-reduce(f32[8,96,2048]{2,1,0:T(8,128)} %bitcast.338, f32[8,96,2048]{2,1,0:T(8,128)} %fusion.37), channel_id=1, replica_groups=mesh['fsdp'=2,'ctx'=8,'tp'=8] {'tp'}, use_global_device_ids=true, to_apply=%region_26.31 | all-reduce | flops 3145728 | bytes 18874368 | tf_op jit(solution)/shard_map/psum | solution.py:146
  787.7 43.2 %all_to_all.40 = bf16[8,96,2048]{2,1,0:T(8,128)(2,1)} all-to-all(bf16[8,96,2048]{2,1,0:T(8,128)(2,1)} %get-tuple-element.157), channel_id=1, replica_groups=mesh['fsdp'=2,'ctx'=8,'tp'=8] {'ctx'}, dimensions={0} | all-to-all | bytes 6291456 | tf_op jit(solution)/shard_map/all_to_all | solution.py:147
  859.9 15.8 all-to-all-done.3
  904.1 11.0 multiply_reduce_fusion.3
  935.4 39.7 %all-to-all-done.6 = bf16[8,96,2048]{2,1,0:T(8,128)(2,1)} async-done(((bf16[8,96,2048]{2,1,0:T(8,128)(2,1)}), bf16[8,96,2048]{2,1,0:T(8,128)(2,1)}, u32[]{:S(2)}, u32[]{:S(2)}) %all-to-all-start.6) | async-done | bytes 3145760 | tf_op jit(solution)/shard_map/all_to_all | solution.py:141
  988.2 12.3 multiply_reduce_fusion
  1000.4 13.4 multiply_convert_fusion
  1104.7 81.8 %all-reduce.12 = bf16[8,96,2048]{2,1,0:T(8,128)(2,1)} all-reduce(f32[8,96,2048]{2,1,0:T(8,128)} %fusion.69), channel_id=1, replica_groups=mesh['fsdp'=2,'ctx'=8,'tp'=8] {'tp'}, use_global_device_ids=true, to_apply=%region_34.39 | all-reduce | flops 1572864 | bytes 9437184 | tf_op jit(solution)/shard_map/psum | solution.py:146
  1201.6 12.2 multiply_reduce_fusion.5
  1232.8 37.2 %reduce-scatter.27.cloned.1.call-done = bf16[128,8]{1,0:T(8,128)(2,1)} async-done(((bf16[2048,8]{1,0:T(8,128)(2,1)}), bf16[128,8]{1,0:T(8,128)(2,1)}) %reduce-scatter.27.cloned.1.call-update) | async-done | bytes 2064
  1271.5 78.9 %reduce-scatter.23.cloned.1.call-done = bf16[704,1024]{1,0:T(8,128)(2,1)} async-done(((bf16[704,2048]{1,0:T(8,128)(2,1)}), bf16[704,1024]{1,0:T(8,128)(2,1)}) %reduce-scatter.23.cloned.1.call-update) | async-done | bytes 1441808 | tf_op jit(solution)/shard_map/reduce_scatter | solution.py:329
  1353.6 23.5 %reduce-scatter.19.cloned.1.call-done = bf16[256,1024]{1,0:T(8,128)(2,1)} async-done(((bf16[256,2048]{1,0:T(8,128)(2,1)}), bf16[256,1024]{1,0:T(8,128)(2,1)}) %reduce-scatter.19.cloned.1.call-update) | async-done | bytes 524304 | tf_op jit(solution)/shard_map/reduce_scatter | solution.py:323
  1379.3 24.7 %reduce-scatter.17.cloned.1.call-done = bf16[1024,256]{1,0:T(8,128)(2,1)} async-done(((bf16[2048,256]{1,0:T(8,128)(2,1)}), bf16[1024,256]{1,0:T(8,128)(2,1)}) %reduce-scatter.17.cloned.1.call-update) | async-done | bytes 524304 | tf_op jit(solution)/shard_map/reduce_scatter | solution.py:320
  1429.3 12.1 multiply_reduce_fusion.1
  1441.4 40.5 %reduce-scatter.21.cloned.1.call-done = bf16[2,1024,704]{1,2,0:T(8,128)(2,1)} async-done(((bf16[2,2048,704]{1,2,0:T(8,128)(2,1)}), bf16[2,1024,704]{1,2,0:T(8,128)(2,1)}) %reduce-scatter.21.cloned.1.call-update) | async-done | bytes 2883600 | tf_op jit(solution)/shard_map/reduce_scatter | solution.py:326
  1487.0 60.3 %all-reduce.9.cloned.1.call-done = bf16[384,2048]{1,0:T(8,128)(2,1)} async-done(((bf16[384,2048]{1,0:T(8,128)(2,1)}), bf16[384,2048]{1,0:T(8,128)(2,1)}) %all-reduce.9.cloned.1.call-update) | async-done | bytes 1572880 | tf_op jit(solution)/shard_map/psum | solution.py:314
  1554.4 34.9 %all-reduce.3 = (bf16[2048]{0:T(1024)(128)(2,1)S(1)}, bf16[2048]{0:T(1024)(128)(2,1)S(1)}) all-reduce(bf16[2048]{0:T(1024)(128)(2,1)S(1)} %get-tuple-element.151, bf16[2048]{0:T(1024)(128)(2,1)S(1)} %copy-done.56), channel_id=7, replica_groups=mesh['fsdp'=2,'ctx'=8,'tp'=8] {'fsdp','ctx'}, use_global_device_ids=true, to_apply=%region_40.45.clone | all-reduce | flops 4096 | bytes 16384
  1595.5 26.5 %reduce-scatter.31.cloned.1.call-done = bf16[128,512]{1,0:T(8,128)(2,1)} async-done(((bf16[2048,512]{1,0:T(8,128)(2,1)}), bf16[128,512]{1,0:T(8,128)(2,1)}) %reduce-scatter.31.cloned.1.call-update) | async-done | bytes 131088
  (401 shorter events, 503.1 us)
Async XLA Ops:
  7.2 525.2 %copy-start = (f32[2048,8]{0,1:T(8,128)S(1)}, f32[2048,8]{0,1:T(8,128)}, u32[]{:S(2)}) copy-start(f32[2048,8]{0,1:T(8,128)} %param.25) | copy-start | bytes 196612
  7.2 68.7 %all-gather.11.cloned.1.call-start = ((), (), s32[]{:S(2)}) async-start(), calls=%async_computation.16 | async-start | bytes 2228224 | tf_op jit(solution)/shard_map/all_gather | solution.py:96
  9.1 247.8 %all-gather.15.cloned.1.call-start = ((), (), s32[]{:S(2)}) async-start(), calls=%async_computation.23 | async-start | bytes 1572864 | tf_op jit(solution)/shard_map/all_gather | solution.py:98
  9.8 264.3 %all-gather.13.cloned.1.call-start = ((), (), s32[]{:S(2)}) async-start(), calls=%async_computation.17 | async-start | bytes 3538944 | tf_op jit(solution)/shard_map/all_gather | solution.py:174
  14.0 453.6 %copy-start.1 = (bf16[384,2048]{1,0:T(8,128)(2,1)}, bf16[384,2048]{1,0:T(8,128)(2,1)S(1)}, u32[]{:S(2)}) copy-start(bf16[384,2048]{1,0:T(8,128)(2,1)S(1)} %fusion.24) | copy-start | bytes 4718596
  108.2 69.8 %copy-start.27 = (s32[8,384,2]{1,2,0:T(2,128)}, s32[8,384,2]{1,2,0:T(2,128)S(1)}, u32[]{:S(2)}) copy-start(s32[8,384,2]{1,2,0:T(2,128)S(1)} %get-tuple-element.181) | copy-start | bytes 73732
  112.7 69.7 %copy-start.65 = (s32[2]{0:T(128)S(1)}, s32[2]{0:T(128)}, u32[]{:S(2)}) copy-start(s32[2]{0:T(128)} %constant.193) | copy-start | bytes 28
  112.7 70.0 %copy-start.64 = (s32[2]{0:T(128)S(1)}, s32[2]{0:T(128)}, u32[]{:S(2)}) copy-start(s32[2]{0:T(128)} %constant.190) | copy-start | bytes 28
  241.4 28.7 %all-to-all-start = ((bf16[8,96,2048]{2,1,0:T(8,128)(2,1)}), bf16[8,96,2048]{2,1,0:T(8,128)(2,1)}, u32[]{:S(2)}, u32[]{:S(2)}) async-start(bf16[8,96,2048]{2,1,0:T(8,128)(2,1)} %bitcast.331), calls=%async_computation | async-start | bytes 6291456 | tf_op jit(solution)/shard_map/all_to_all | solution.py:141
  246.8 61.7 %all-gather.17.cloned.1.call-start = ((), (), s32[]{:S(2)}) async-start(), calls=%async_computation.24 | async-start | bytes 1572864 | tf_op jit(solution)/shard_map/all_gather | solution.py:99
  247.4 327.2 %all-gather.19.cloned.1.call-start = ((), (), s32[]{:S(2)}) async-start(), calls=%async_computation.25 | async-start | bytes 8650752 | tf_op jit(solution)/shard_map/all_gather | solution.py:100
  252.3 160.8 %copy-start.29 = (s32[8,384,2]{1,2,0:T(2,128)}, s32[8,384,2]{1,2,0:T(2,128)S(1)}, u32[]{:S(2)}) copy-start(s32[8,384,2]{1,2,0:T(2,128)S(1)} %copy.301) | copy-start | bytes 73732
  253.6 210.9 %copy-start.46 = (pred[8,384,2]{1,2,0:T(4,128)(4,1)}, pred[8,384,2]{1,2,0:T(4,128)(4,1)S(1)}, u32[]{:S(2)}) copy-start(pred[8,384,2]{1,2,0:T(4,128)(4,1)S(1)} %broadcast_compare_fusion) | copy-start | bytes 18436
  405.4 69.4 %all-to-all-start.1 = ((bf16[8,96,2048]{2,1,0:T(8,128)(2,1)}), bf16[8,96,2048]{2,1,0:T(8,128)(2,1)}, u32[]{:S(2)}, u32[]{:S(2)}) async-start(bf16[8,96,2048]{2,1,0:T(8,128)(2,1)} %all-reduce.10), calls=%async_computation.1 | async-start | bytes 6291456 | tf_op jit(solution)/shard_map/all_to_all | solution.py:147
  517.7 46.7 %all-to-all-start.2 = ((bf16[8,96,2048]{2,1,0:T(8,128)(2,1)}), bf16[8,96,2048]{2,1,0:T(8,128)(2,1)}, u32[]{:S(2)}, u32[]{:S(2)}) async-start(bf16[8,96,2048]{2,1,0:T(8,128)(2,1)} %bitcast.330), calls=%async_computation.2 | async-start | bytes 6291456 | tf_op jit(solution)/shard_map/all_to_all | solution.py:141
  524.5 101.5 %all-gather.21.cloned.1.call-start = ((), (), s32[]{:S(2)}) async-start(), calls=%async_computation.26 | async-start | bytes 4325376 | tf_op jit(solution)/shard_map/all_gather | solution.py:101
  564.4 61.6 %all-to-all-start.4 = ((bf16[8,96,2048]{2,1,0:T(8,128)(2,1)}), bf16[8,96,2048]{2,1,0:T(8,128)(2,1)}, u32[]{:S(2)}, u32[]{:S(2)}) async-start(bf16[8,96,2048]{2,1,0:T(8,128)(2,1)} %bitcast.332), calls=%async_computation.4 | async-start | bytes 6291456 | tf_op jit(solution)/shard_map/all_to_all | solution.py:141
  830.9 44.9 %all-to-all-start.3 = ((bf16[8,96,2048]{2,1,0:T(8,128)(2,1)}), bf16[8,96,2048]{2,1,0:T(8,128)(2,1)}, u32[]{:S(2)}, u32[]{:S(2)}) async-start(bf16[8,96,2048]{2,1,0:T(8,128)(2,1)} %get-tuple-element.158), calls=%async_computation.3 | async-start | bytes 6291456 | tf_op jit(solution)/shard_map/all_to_all | solution.py:147
  930.7 44.4 %all-to-all-start.6 = ((bf16[8,96,2048]{2,1,0:T(8,128)(2,1)}), bf16[8,96,2048]{2,1,0:T(8,128)(2,1)}, u32[]{:S(2)}, u32[]{:S(2)}) async-start(bf16[8,96,2048]{2,1,0:T(8,128)(2,1)} %bitcast.333), calls=%async_computation.6 | async-start | bytes 6291456 | tf_op jit(solution)/shard_map/all_to_all | solution.py:141
  935.3 260.1 %reduce-scatter.25.cloned.1.call-start = ((), (), s32[]{:S(2)}) async-start(), calls=%async_computation.27 | async-start | bytes 3538944
  1024.1 207.3 %reduce-scatter.29.cloned.1.call-start = ((), (), s32[]{:S(2)}) async-start(), calls=%async_computation.29 | async-start | bytes 557056
  1047.5 222.6 %reduce-scatter.27.cloned.1.call-start = ((), (), s32[]{:S(2)}) async-start(), calls=%async_computation.28 | async-start | bytes 557056
  1050.7 299.6 %reduce-scatter.23.cloned.1.call-start = ((), (), s32[]{:S(2)}) async-start(), calls=%async_computation.22 | async-start | bytes 4325376 | tf_op jit(solution)/shard_map/reduce_scatter | solution.py:329
  1058.0 319.2 %reduce-scatter.19.cloned.1.call-start = ((), (), s32[]{:S(2)}) async-start(), calls=%async_computation.20 | async-start | bytes 1572864 | tf_op jit(solution)/shard_map/reduce_scatter | solution.py:323
  1062.1 341.9 %reduce-scatter.17.cloned.1.call-start = ((), (), s32[]{:S(2)}) async-start(), calls=%async_computation.19 | async-start | bytes 1572864 | tf_op jit(solution)/shard_map/reduce_scatter | solution.py:320
  1075.0 406.9 %reduce-scatter.21.cloned.1.call-start = ((), (), s32[]{:S(2)}) async-start(), calls=%async_computation.21 | async-start | bytes 8650752 | tf_op jit(solution)/shard_map/reduce_scatter | solution.py:326
  1186.6 219.5 %all-to-all-start.7 = ((bf16[8,96,2048]{2,1,0:T(8,128)(2,1)}), bf16[8,96,2048]{2,1,0:T(8,128)(2,1)}, u32[]{:S(2)}, u32[]{:S(2)}) async-start(bf16[8,96,2048]{2,1,0:T(8,128)(2,1)} %all-reduce.12), calls=%async_computation.7 | async-start | bytes 6291456 | tf_op jit(solution)/shard_map/all_to_all | solution.py:147
  1195.4 351.9 %all-reduce.9.cloned.1.call-start = ((), (), s32[]{:S(2)}) async-start(), calls=%async_computation.18 | async-start | bytes 3145728 | tf_op jit(solution)/shard_map/psum | solution.py:314
  1201.3 420.6 %reduce-scatter.31.cloned.1.call-start = ((), (), s32[]{:S(2)}) async-start(), calls=%async_computation.30 | async-start | bytes 2228224
  1271.5 134.6 %copy-start.40 = (s32[1024]{0:T(1024)S(1)}, s32[1024]{0:T(1024)}, u32[]{:S(2)}) copy-start(s32[1024]{0:T(1024)} %copy-done.39) | copy-start | bytes 12292
  1441.3 105.9 %copy-start.26 = (f32[2048,8]{0,1:T(8,128)S(1)}, f32[2048,8]{0,1:T(8,128)}, u32[]{:S(2)}) copy-start(f32[2048,8]{0,1:T(8,128)} %param.24) | copy-start | bytes 196612
  1487.0 103.5 %copy-start.62 = (f32[384]{0:T(512)S(1)}, f32[384]{0:T(512)}, u32[]{:S(2)}) copy-start(f32[384]{0:T(512)} %get-tuple-element.183) | copy-start | bytes 4612
  (59 other events, 713.5 us)
Sparse Core Ops, SparseCore 0:
  10.2 65.6 all-gather.10
  77.5 34.7 all-gather.14
  115.1 67.8 all-gather.12
  249.0 50.6 all-gather.16
  301.2 77.6 all-gather.18
  526.7 99.3 all-gather.20
  1024.2 94.3 reduce-scatter.24
  1121.0 65.2 reduce-scatter.28
  1188.7 81.3 reduce-scatter.26
  1272.9 77.3 reduce-scatter.22
  1353.3 23.8 reduce-scatter.18
  1380.0 23.8 reduce-scatter.16
  1407.0 74.8 reduce-scatter.20
  1484.2 62.9 all-reduce.8
  1549.6 72.2 reduce-scatter.30
where the time goes:
time: 1650 us; the launch traced here: 1630 us
  waiting for transfers between devices  477 us (29%)
  blocking collectives  412 us (25%)
  local copies, waits for them, and re-layouts  306 us (19%)
  other arithmetic  214 us (13%)
  matrix products  156 us (9%)
  starting transfers between devices  50 us (3%)
    psum x3, blocking collectives, to_home(): summed = lax.psum(partial_rows, 'tp')  306 us
    unnamed x165, local copies, waits for them, and re-layouts  128 us
    reduce_scatter x1, waiting for transfers between devices, local(): lax.psum_scatter(down_grad.astype(jnp.bfloat16), 'fsdp', scatter_dimensio...  78.9 us
    all_to_all x4, waiting for transfers between devices, to_experts(): lax.all_to_all(home_rows, 'ctx', split_axis=0, concat_axis=0, tiled=True)  68.4 us
    unnamed x19, waiting for transfers between devices  65.8 us
    all_gather x1, waiting for transfers between devices, local(): kv_full = lax.all_gather(kv_weight, ('fsdp', 'ctx'), axis=1, tiled=True)  61.9 us
    psum x1, waiting for transfers between devices, local(): lax.psum(grad_lowered_kv.astype(jnp.bfloat16), 'tp').astype(jnp.float32)  60.3 us
    another operation x4, other arithmetic  50.8 us
  transfers between devices with their start and end apart: 22, of which 13 were waited for; matrix products, arithmetic and copies ran while one was open for 33% of the time, Pallas kernels for 0%

commit v1 on v0

v1 whole, which is shorter than its diff:
```python
from functools import partial

import jax
import jax.numpy as jnp
from jax import lax
from jax.experimental import pallas as pl
from jax.experimental.pallas import tpu as pltpu
from jax.sharding import PartitionSpec as P

MESH = pl.DeviceIdType.MESH
HD = 128
CTX = 8
TP = 8
FSDP = 2
VLIM = 61 * 1024 * 1024
epsilon = 1e-06
masked_score = -1e30
f32 = jnp.float32
bf16 = jnp.bfloat16
DMA = pltpu.SemaphoreType.DMA
VM = pltpu.VMEM


def vmem(n):
    return [pl.BlockSpec(memory_space=pltpu.VMEM)] * n


def anywhere(n):
    return [pl.BlockSpec(memory_space=pl.ANY)] * n


def params(cid=None):
    if cid is None:
        return pltpu.CompilerParams(vmem_limit_bytes=VLIM)
    return pltpu.CompilerParams(collective_id=cid, has_side_effects=True, vmem_limit_bytes=VLIM)


def cost(us):
    return pl.CostEstimate(flops=0, bytes_accessed=int(us * 3.2e6), transcendentals=0)


def sds(shape, dtype):
    return jax.ShapeDtypeStruct(shape, dtype)


def nt(a, b):
    return lax.dot_general(a, b, (((1,), (1,)), ((), ())), preferred_element_type=f32)


def tn(a, b):
    return lax.dot_general(a, b, (((0,), (0,)), ((), ())), preferred_element_type=f32)


def nn(a, b):
    return jnp.dot(a, b, preferred_element_type=f32)


def wide(v):
    return v.astype(f32)


class Place:
    def __init__(self):
        self.f, self.c, self.t = lax.axis_index("fsdp"), lax.axis_index("ctx"), lax.axis_index("tp")
        self.x, self.k = self.t // 2, lax.rem(self.t, 2)
        self.xl, self.xr, self.xo = (lax.rem(self.x + i, 4) for i in (3, 1, 2))
        self.right, self.left = {"tp": self.xr * 2 + self.k}, {"tp": self.xl * 2 + self.k}
        self.sib = {"tp": self.x * 2 + 1 - self.k}
        self.zh, self.y = self.c // 4, lax.rem(self.c, 4)
        self.z = self.zh * 2 + self.f
        self.up, self.down = ({"ctx": self.zh * 4 + lax.rem(self.y + i, 4)} for i in (1, 3))
        self.across = {"ctx": lax.rem(self.c + 4, CTX)}
        self.partner = {"fsdp": 1 - self.f}
        self.above, self.below = (self.at_z(lax.rem(self.z + i, 4)) for i in (1, 3))

    def at_z(self, z):
        return {"fsdp": lax.rem(z, 2), "ctx": (z // 2) * 4 + self.y}

    def ctx_peers(self):
        return [{"ctx": lax.rem(self.c + j, CTX)} for j in range(1, CTX)]

    def tp_near(self):
        return [self.right, self.left, self.sib]

    def z_near(self):
        return [self.above, self.below]


def greet(peers):
    barrier = pltpu.get_barrier_semaphore()
    for axes in peers:
        pl.semaphore_signal(barrier, inc=1, device_id=axes, device_id_type=MESH)
    pl.semaphore_wait(barrier, len(peers))


class Net:
    def __init__(self, send, recv):
        self.send, self.recv, self.used, self.open = send, recv, 0, []

    def go(self, src, dst, axes):
        i = self.used
        self.used += 1
        d = pltpu.make_async_remote_copy(
            src_ref=src, dst_ref=dst, send_sem=self.send.at[i], recv_sem=self.recv.at[i],
            device_id=axes, device_id_type=MESH,
        )
        d.start()
        self.open.append(d)
        return d

    def drain(self):
        for d in self.open:
            d.wait_send()
        self.open = []


class Ring:
    def __init__(self, net, view, me, plus, minus):
        self.net, self.view, self.plus, self.minus = net, view, plus, minus
        self.me, self.low, self.high, self.far = me, lax.rem(me + 3, 4), lax.rem(me + 1, 4), lax.rem(me + 2, 4)

    def hop1(self, src=None):
        src = self.view(self.me, None) if src is None else src
        self.a = self.net.go(src, self.view(self.me, None), self.plus)
        self.b = self.net.go(src, self.view(self.me, None), self.minus)

    def hop2_low(self):
        self.a.wait_recv()
        self.a = self.net.go(self.view(self.low, 0), self.view(self.low, 0), self.plus)

    def hop2_high(self):
        self.b.wait_recv()
        self.b = self.net.go(self.view(self.high, 1), self.view(self.high, 1), self.minus)

    def hop2(self):
        self.hop2_low()
        self.hop2_high()

    def hop3(self):
        self.a.wait_recv()
        self.b.wait_recv()


class RingSum:
    def __init__(self, net, own, stage, land, me, plus, minus):
        self.net, self.own, self.stage, self.land, self.plus, self.minus = net, own, stage, land, plus, minus
        self.me, self.low, self.high, self.far = me, lax.rem(me + 3, 4), lax.rem(me + 1, 4), lax.rem(me + 2, 4)

    def put(self, position, part, value):
        r = self.stage(position, part)
        r[...] = value.astype(r.dtype)
        return r

    def hop1(self):
        self.a = self.net.go(self.put(self.far, 0, self.own(self.far, 0)), self.land("a"), self.plus)
        self.b = self.net.go(self.put(self.far, 1, self.own(self.far, 1)), self.land("b"), self.minus)

    def hop2(self):
        self.a.wait_recv()
        self.put(self.high, 0, self.own(self.high, 0) + wide(self.land("a")[...]))
        self.put(self.high, 1, self.own(self.high, 1))
        self.a = self.net.go(self.stage(self.high, None), self.land("l"), self.plus)
        self.b.wait_recv()
        self.put(self.low, 1, self.own(self.low, 1) + wide(self.land("b")[...]))
        self.put(self.low, 0, self.own(self.low, 0))
        self.b = self.net.go(self.stage(self.low, None), self.land("r"), self.minus)

    def hop3(self):
        self.a.wait_recv()
        self.b.wait_recv()
        return self.own(self.me, None) + wide(self.land("l")[...]) + wide(self.land("r")[...])


def part_of(part, size):
    half = size // 2
    return pl.ds(0, size) if part is None else pl.ds(part * half, half)


class Dispatch:
    def __init__(self, net, at, x_ref, o_ref, exchange=True):
        self.net, self.at, self.x_ref, self.o_ref, self.exchange = net, at, x_ref, o_ref, exchange
        self.n, self.rows, self.w = x_ref.shape

    def view(self, block, tt, part=None):
        half = self.rows // 2
        lo, size = (0, self.rows) if part is None else (part * half, half)
        row = pl.multiple_of(block * self.rows + lo, 16)
        return self.o_ref.at[pl.ds(row, size), pl.ds(pl.multiple_of(tt * self.w, self.w), self.w)]

    def start(self):
        c, n = self.at.c, self.n
        if self.exchange:
            self.blocks = [lax.rem(c + n - j, n) for j in range(n)]
            self.moves = [None]
            for j in range(1, n):
                e = lax.rem(c + j, n)
                self.moves.append(self.net.go(self.x_ref.at[e], self.view(c, self.at.t), {"ctx": e}))
            self.view(c, self.at.t)[...] = self.x_ref[c]
        else:
            self.blocks, self.moves = list(range(n)), [None] * n
            for j in range(n):
                self.view(j, self.at.t)[...] = self.x_ref[j]

    def sibling(self, b, tt):
        return self.net.go(self.view(b, tt), self.view(b, tt), self.at.sib)

    def hop1(self):
        at = self.at
        self.rings, self.sibs = [], []
        for b, move in zip(self.blocks, self.moves):
            if move is not None:
                move.wait_recv()
            ring = Ring(self.net, lambda xx, part, b=b: self.view(b, xx * 2 + at.k, part), at.x, at.right, at.left)
            ring.hop1()
            self.rings.append(ring)
            self.sibs.append(self.sibling(b, at.t))

    def hop2(self):
        at = self.at
        for b, ring in zip(self.blocks, self.rings):
            ring.hop2_low()
            self.sibs.append(self.sibling(b, at.xl * 2 + at.k))
            ring.hop2_high()
            self.sibs.append(self.sibling(b, at.xr * 2 + at.k))

    def hop3(self):
        at = self.at
        for b, ring in zip(self.blocks, self.rings):
            ring.hop3()
            self.sibs.append(self.sibling(b, at.xo * 2 + at.k))

    def finish(self):
        for s in self.sibs:
            s.wait_recv()

    COPIES = 8 * 9 + 7


class Collect:
    def __init__(self, net, at, p_ref, o_ref, sibbuf, abuf, bbuf, lbuf, rbuf, fbuf, exchange=True):
        self.net, self.at, self.p, self.o, self.exchange = net, at, p_ref, o_ref, exchange
        self.sibbuf, self.fbuf = sibbuf, fbuf
        self.lands = {"a": abuf, "b": bbuf, "l": lbuf, "r": rbuf}
        _, _, self.n, self.rows, self.w = p_ref.shape
        n, c = self.n, at.c
        self.blocks = [lax.rem(c + j, n) for j in range(1, n)] + [c] if exchange else list(range(n))

    def start(self, which=None):
        at = self.at
        self.sibs = [self.net.go(self.p.at[1 - at.k, :, b], self.sibbuf.at[:, b], at.sib) for b in self.blocks]

    def own(self, b, xx, part):
        s = part_of(part, self.rows)
        return wide(self.p[self.at.k, xx, b, s]) + wide(self.sibbuf[xx, b, s])

    def hop1(self):
        at = self.at
        self.rings = []
        for b, sib in zip(self.blocks, self.sibs):
            sib.wait_recv()
            ring = RingSum(
                self.net,
                partial(self.own, b),
                lambda xx, part, b=b: self.fbuf.at[xx, b, part_of(part, self.rows)],
                lambda name, b=b: self.lands[name].at[b],
                at.x, at.right, at.left,
            )
            ring.hop1()
            self.rings.append(ring)

    def hop2(self):
        for ring in self.rings:
            ring.hop2()

    def hop3(self):
        at = self.at
        self.moves = []
        for j, (b, ring) in enumerate(zip(self.blocks, self.rings)):
            total = ring.hop3()
            if self.exchange and j < self.n - 1:
                self.fbuf[at.x, b] = total.astype(self.fbuf.dtype)
                self.moves.append(self.net.go(self.fbuf.at[at.x, b], self.o.at[at.c, pl.ds(0, self.rows)], {"ctx": b}))
            else:
                self.o[b, pl.ds(0, self.rows)] = total.astype(self.o.dtype)

    def finish(self):
        for m in self.moves:
            m.wait_recv()

    COPIES = 8 * 5 + 7

    @staticmethod
    def scratch(n, rows, w):
        return [
            VM((4, n, rows, w), bf16), VM((n, rows // 2, w), bf16), VM((n, rows // 2, w), bf16),
            VM((n, rows, w), bf16), VM((n, rows, w), bf16), VM((4, n, rows, w), bf16),
        ]


def sems(n):
    return [DMA((n,)), DMA((n,))]


def exact(a, b):
    return jnp.dot(a, b, preferred_element_type=f32, precision=lax.Precision.HIGHEST)


def split3(v):
    high = v.astype(bf16)
    rest = v - wide(high)
    mid = rest.astype(bf16)
    return high, mid, (rest - wide(mid)).astype(bf16)


def three_rows(v):
    high, mid, low = split3(v)
    row = lax.broadcasted_iota(jnp.int32, (8, v.shape[1]), 0)
    pieces = jnp.where(row == 0, wide(high), jnp.where(row == 1, wide(mid), jnp.where(row == 2, wide(low), 0.0)))
    return pieces.astype(bf16)


def to_row_form(columns, rows):
    return columns.T[:rows]


def to_column_form(rows):
    fill = jnp.zeros((128 - rows.shape[0], rows.shape[1]), f32)
    return jnp.concatenate([rows, fill], axis=0).T


def route_columns(routes):
    row = lax.broadcasted_iota(jnp.int32, (8, routes.shape[1]), 0)
    both = jnp.where(row == 0, routes[0:1, :], jnp.where(row == 1, routes[1:2, :], 0)).astype(f32)
    columns = to_column_form(both)
    return columns[:, 0:1], columns[:, 1:2]


FIRST = 8


def hot_lanes(routes):
    lane = lax.broadcasted_iota(jnp.int32, (routes.shape[1], 128), 1).astype(f32)
    return [(lane == r + FIRST).astype(f32) for r in route_columns(routes)]


def pick_matrix(routes, cap):
    tok = routes.shape[1]
    lane = lax.broadcasted_iota(jnp.int32, (tok, 128), 1).astype(f32)
    columns = route_columns(routes)
    hot = [(lane == r).astype(f32) for r in columns]
    row = lax.broadcasted_iota(jnp.int32, (tok, tok), 0)
    col = lax.broadcasted_iota(jnp.int32, (tok, tok), 1)
    earlier = (col < row).astype(f32).astype(bf16)
    before = nn(earlier, (hot[0] + hot[1]).astype(bf16))
    slot = lax.broadcasted_iota(jnp.int32, (tok, CTX * 128), 1).astype(f32)
    out = []
    for r, o in zip(columns, hot):
        place = jnp.sum(before * o, axis=1, keepdims=True)
        target = jnp.where(place < cap, r * 128 + place, -1.0)
        out.append((slot == target).astype(f32).astype(bf16))
    return out


def pair_positions(pos_ref, g, cap):
    a, b = wide(pos_ref[2 * g]), wide(pos_ref[2 * g + 1])
    none = jnp.zeros_like(a)
    lane = lax.broadcasted_iota(jnp.int32, (a.shape[0], 256), 1)
    a = jnp.concatenate([a, none], axis=1)
    b = pltpu.roll(jnp.concatenate([b, none], axis=1), cap, 1)
    return jnp.where(lane < cap, a, b)[0:1, : 2 * cap].astype(jnp.int32)


def front_body(
    tokens, norm_in, router_t, routes_att, routes_mlp, cot, kv_w, q_own, o_own, gu_own,
    rows_att, rows_g, kv_seq, kv_full, pos_out, lowered, pick_att, pick_mlp, info, q_oth, o_oth, gu_oth,
    slots_att, slots_g, pos, send, recv,
):
    at, net = Place(), Net(send, recv)
    tok, width = tokens.shape
    kv_part, w = kv_w.shape[1:]
    cap, part = slots_att.shape[1:]

    def kvw(z, y, p):
        return kv_full.at[lax.rem(z, 2) * CTX + (z // 2) * 4 + y, part_of(p, kv_part)]

    own = kvw(at.z, at.y, None)
    own[:, :w] = kv_w[0]
    own[:, w:] = kv_w[1]
    greet(at.ctx_peers() + at.tp_near() + at.z_near())
    zring = Ring(net, lambda z, p: kvw(z, at.y, p), at.z, at.above, at.below)
    zring.hop1()
    moves = [net.go(q_own, q_oth, at.partner)]
    yrings = []

    def y_stage(z):
        ring = Ring(net, lambda y, p: kvw(z, y, p), at.y, at.up, at.down)
        ring.hop1()
        yrings.append(ring)

    y_stage(at.z)
    for i, r in enumerate(pick_matrix(routes_att[...], cap)):
        pick_att[i * tok : (i + 1) * tok, :] = r
    zring.hop2()
    y_stage(zring.low)
    y_stage(zring.high)
    x = wide(tokens[...])
    scale = lax.rsqrt(jnp.sum(x * x, axis=1, keepdims=True) / width + epsilon)
    lowered[...] = (x * scale * norm_in[...]).astype(bf16)
    mine = pl.ds(pl.multiple_of(at.t * part, part), part)
    both = pick_att[:tok, :] + pick_att[tok:, :]
    slots = tn(both, lowered[:, mine]).astype(bf16)
    for e in range(CTX):
        slots_att[e] = slots[e * 128 : e * 128 + cap]
    d_att = Dispatch(net, at, slots_att, rows_att)
    d_att.start()
    number = lax.broadcasted_iota(jnp.int32, (8, tok), 1)
    row = lax.broadcasted_iota(jnp.int32, (8, tok), 0)
    digits = jnp.where(row == 0, number // 16, jnp.where(row == 1, lax.rem(number, 16), 0)).astype(f32).astype(bf16)
    found = nn(digits, both)
    found = (found[0:1] * 16.0 + found[1:2]).astype(jnp.int32) + at.c * tok
    for e in range(CTX):
        pos[e] = jnp.broadcast_to(found[:, e * 128 : (e + 1) * 128], (8, 128))
    for j in range(1, CTX):
        e = lax.rem(at.c + j, CTX)
        moves.append(net.go(pos.at[e], pos_out.at[at.c], {"ctx": e}))
    pos_out[at.c] = pos[at.c]
    for i, r in enumerate(pick_matrix(routes_mlp[...], cap)):
        pick_mlp[i * tok : (i + 1) * tok, :] = r
    slots = tn(pick_mlp[:tok, :] + pick_mlp[tok:, :], cot[:, mine]).astype(bf16)
    for e in range(CTX):
        slots_g[e] = slots[e * 128 : e * 128 + cap]
    d_g = Dispatch(net, at, slots_g, rows_g)
    d_g.start()
    d_att.hop1()
    zring.hop3()
    y_stage(zring.far)
    logits = sum(nt(r, lowered[...]) for r in split3(router_t[...]))
    columns = to_column_form(jnp.concatenate([jnp.zeros_like(logits), logits], axis=0))
    hot = hot_lanes(routes_att[...])
    low = [jnp.sum(o * columns, axis=1, keepdims=True) for o in hot]
    lane = lax.broadcasted_iota(jnp.int32, (tok, 128), 1)
    g0 = 1.0 / (1.0 + jnp.exp(low[1] - low[0]))
    g1 = 1.0 / (1.0 + jnp.exp(low[0] - low[1]))
    info[...] = jnp.where(
        lane == 0, scale, jnp.where(lane == 1, g0, jnp.where(lane == 2, g1, columns / scale))
    )
    d_att.hop2()
    for ring in yrings:
        ring.hop2()
    d_g.hop1()
    for ring in yrings:
        ring.hop3()
    weights = kv_full[...].reshape(-1, 2 * w)
    kv_seq[at.c] = nn(lowered[...], weights).astype(bf16)
    over = net.go(kv_seq.at[at.c], kv_seq.at[at.c], at.across)

    def seq_ring(zh):
        return Ring(net, lambda y, p: kv_seq.at[zh * 4 + y, part_of(p, tok)], at.y, at.up, at.down)

    near, far = seq_ring(at.zh), seq_ring(1 - at.zh)
    near.hop1()
    moves.append(net.go(o_own, o_oth, at.partner))
    rows = gu_oth.shape[1]
    moves.append(net.go(gu_own.at[:, pl.ds(0, rows)], gu_oth, at.partner))
    d_att.hop3()
    d_g.hop2()
    over.wait_recv()
    far.hop1()
    d_att.finish()
    near.hop2()
    d_g.hop3()
    near.hop3()
    far.hop2()
    d_g.finish()
    far.hop3()
    for m in moves:
        m.wait_recv()
    net.drain()


def front(tokens, norm_in, router_t, routes_att, routes_mlp, cot, kv_w, q_own, o_own, gu_own, cap, chunk, cid):
    tok, width = tokens.shape
    part = width // TP
    _, kv_part, w = kv_w.shape
    wide_rows = sds((CTX * cap, width), bf16)
    pick = sds((2 * tok, CTX * 128), bf16)
    return pl.pallas_call(
        front_body,
        out_shape=(
            wide_rows, wide_rows, sds((CTX, tok, 2 * w), bf16), sds((FSDP * CTX, kv_part, 2 * w), bf16),
            sds((CTX, 8, 128), jnp.int32), sds((tok, width), bf16), pick, pick, sds((tok, 128), f32),
            sds(q_own.shape, bf16), sds(o_own.shape, bf16), sds((2, chunk, gu_own.shape[2]), bf16),
        ),
        in_specs=vmem(7) + anywhere(3),
        out_specs=tuple(vmem(9) + anywhere(3)),
        scratch_shapes=[VM((CTX, cap, part), bf16), VM((CTX, cap, part), bf16), VM((CTX, 8, 128), jnp.int32)]
        + sems(2 * Dispatch.COPIES + 64),
        compiler_params=params(cid),
        cost_estimate=cost(70),
    )(tokens, norm_in, router_t, routes_att, routes_mlp, cot, kv_w, q_own, o_own, gu_own)


def assemble(own, other, full, axis, f, sem):
    size = own.shape[axis]
    out = []
    for i, (src, pos) in enumerate(((own, f), (other, 1 - f))):
        s = pl.ds(pl.multiple_of(pos * size, size), size)
        dst = full.at[s] if axis == 0 else full.at[:, s]
        d = pltpu.make_async_copy(src, dst, sem.at[i])
        d.start()
        out.append(d)
    return out


def attend_body(
    cap, tok, first, rows_ref, q_own, q_oth, o_own, o_oth, kv_ref, pos_ref, gu_own,
    q_ref, att_ref, lse_ref, p_ref, gu_oth,
    wq, wo, vt_ref, local_sem, send, recv,
):
    at, net = Place(), Net(send, recv)
    heads = q_ref.shape[1] // HD
    width = heads * HD
    scale = HD ** (-0.5)
    total = q_ref.shape[0]
    load_q = assemble(q_own, q_oth, wq, 0, at.f, local_sem.at[0])
    load_o = assemble(o_own, o_oth, wo, 1, at.f, local_sem.at[1])
    greet([at.partner])
    chunk = gu_oth.shape[1]
    move = net.go(gu_own.at[:, pl.ds(first, chunk)], gu_oth, at.partner)
    for h in range(heads):
        vt_ref[h] = kv_ref[:, width + h * HD : width + (h + 1) * HD].T
    for d in load_q:
        d.wait()
    q_ref[...] = nn(rows_ref[...], wq[...]).astype(bf16)
    for d in load_o:
        d.wait()
    rows_at, keys_at = 2 * cap, 2 * tok
    for g in range(total // rows_at):
        lo = g * rows_at
        extent = (g + 1) * keys_at
        at_key = extent - keys_at
        pos = pair_positions(pos_ref, g, cap)
        for h in range(heads):
            cols = slice(h * HD, (h + 1) * HD)
            s = nt(kv_ref[:extent, cols], q_ref[lo : lo + rows_at, cols]) * scale
            ids = lax.broadcasted_iota(jnp.int32, (keys_at, rows_at), 0) + at_key
            last = jnp.where(ids <= pos, s[at_key:], masked_score)
            highest = jnp.max(last, axis=0, keepdims=True)
            if g:
                highest = jnp.maximum(highest, jnp.max(s[:at_key], axis=0, keepdims=True))
            e_last = jnp.exp(last - highest)
            sums = jnp.sum(e_last, axis=0, keepdims=True)
            mixed = nn(vt_ref[h, :, at_key:extent], e_last.astype(bf16))
            if g:
                e = jnp.exp(s[:at_key] - highest)
                sums = sums + jnp.sum(e, axis=0, keepdims=True)
                mixed = mixed + nn(vt_ref[h, :, :at_key], e.astype(bf16))
            att_ref[lo : lo + rows_at, cols] = (mixed / sums).T.astype(bf16)
            lse_ref[h : h + 1, lo : lo + rows_at] = highest + jnp.log(sums)
        out = nn(att_ref[lo : lo + rows_at, :], wo[...]).astype(bf16)
        for i in range(TP):
            for b in range(2):
                p_ref[i % 2, i // 2, 2 * g + b] = out[b * cap : (b + 1) * cap, i * width : (i + 1) * width]
    move.wait_recv()
    net.drain()


def attend(rows, q_own, q_oth, o_own, o_oth, kv, pos, gu_own, tok, cap, first, chunk, cid):
    heads = q_own.shape[1] // HD
    slots, width = rows.shape
    w = heads * HD
    return pl.pallas_call(
        partial(attend_body, cap, tok, first),
        out_shape=(
            sds((slots, w), bf16), sds((slots, w), bf16), sds((heads, slots), f32),
            sds((2, 4, slots // cap, cap, width // TP), bf16), sds((2, chunk, gu_own.shape[2]), bf16),
        ),
        in_specs=vmem(1) + anywhere(4) + vmem(2) + anywhere(1),
        out_specs=tuple(vmem(4) + anywhere(1)),
        scratch_shapes=[VM((width, w), bf16), VM((w, width), bf16), VM((heads, HD, kv.shape[0]), bf16), DMA((2, 2))] + sems(1),
        compiler_params=params(cid),
        cost_estimate=cost(25),
    )(rows, q_own, q_oth, o_own, o_oth, kv, pos, gu_own)


def all_peers(at):
    me = at.f * CTX + at.c
    out = []
    for j in range(1, FSDP * CTX):
        p = lax.rem(me + j, FSDP * CTX)
        out.append({"fsdp": p // CTX, "ctx": lax.rem(p, CTX)})
    return out


def tp_peers(at):
    return [{"tp": lax.rem(at.t + j, TP)} for j in range(1, TP)]


def tail_body(
    spans, split,
    p_ref, dkv, lowered, kv_full, mlp_ret, hidden, gates_mlp, pick_mlp, pick_att, att_picked, grad_hidden, info,
    routes, norm_in, router_t, norm_mid_grad, router_mlp_grad, tokens, *refs,
):
    count = len(spans)
    sources, refs = refs[:count], refs[count:]
    parts = list(zip(spans, sources))
    kvw_out, result, input_grad, minor_out = refs[:4]
    outs, refs = refs[4 : 4 + count], refs[4 + count :]
    bufs, refs = refs[:6], refs[6:]
    (stage_near, stage_far, ka, kb, kl, kr, fa, fb, fl, fr, over_out, over_in, kv_low,
     p2, c2_sib, c2_a, c2_b, c2_l, c2_r, c2_f,
     w_part, w_stage, w_half, w_whole, w_sum, wz_stage, wz_half, wz_whole,
     ret, kv_back, slots, x_res, x_in, small_out, small_in, minor, minor_in, minor_sum, rgrad, toks, tok_sem,
     send, recv) = refs
    at, net = Place(), Net(send, recv)
    tok, w = dkv.shape[1:]
    kv_part = kv_full.shape[1]
    part = hidden.shape[1]
    width = part * TP
    cap = mlp_ret.shape[1]
    mine = pl.ds(pl.multiple_of(at.t * part, part), part)
    load = pltpu.make_async_copy(tokens.at[:, mine], toks, tok_sem.at[0])
    load.start()
    ret[...] = jnp.zeros_like(ret)
    near_tp = tp_peers(at)
    far_all = all_peers(at)
    greet(far_all + near_tp)

    def bulk(lo, hi):
        return [net.go(span(src), out, at.partner) for (span, src), out in zip(parts[lo:hi], outs[lo:hi])]

    def seq_sum(zh, stage, lands):
        return RingSum(
            net,
            lambda y, p: wide(dkv[zh * 4 + y, part_of(p, tok)]),
            lambda y, p: stage.at[y, part_of(p, tok)],
            lambda name: lands[name],
            at.y, at.up, at.down,
        )

    moves = bulk(0, split[0])
    far = seq_sum(1 - at.zh, stage_far, {"a": fa, "b": fb, "l": fl, "r": fr})
    near = seq_sum(at.zh, stage_near, {"a": ka, "b": kb, "l": kl, "r": kr})
    far.hop1()
    near.hop1()
    col = Collect(net, at, p_ref, ret, *bufs)
    col.start()
    col.hop1()
    far.hop2()
    near.hop2()
    col.hop2()
    over_out[...] = far.hop3().astype(bf16)
    over = net.go(over_out, over_in, at.across)
    own = near.hop3()
    col.hop3()
    moves += bulk(split[0], split[1])

    for e in range(CTX):
        slots[e * 128 : e * 128 + cap, :] = mlp_ret[e]
        slots[e * 128 + cap : (e + 1) * 128, :] = jnp.zeros((128 - cap, part), bf16)
    picked = nn(pick_mlp[...], slots[...])
    gates = gates_mlp[...]
    value = hidden[...] + gates[:, 0:1] * picked[:tok] + gates[:, 1:2] * picked[tok:]
    x_res[...] = value.astype(bf16).reshape(x_res.shape)
    d_res = Dispatch(net, at, x_res, result, exchange=False)
    d_res.start()
    d_res.hop1()

    over.wait_recv()
    kv_low[...] = (own + wide(over_in[...])).astype(bf16)
    back = nt(kv_low[...], kv_full[...].reshape(-1, w)).astype(bf16)
    n2, rows2, w2 = p2.shape[2:]
    for i in range(TP):
        p2[i % 2, i // 2] = back[:, i * w2 : (i + 1) * w2].reshape(n2, rows2, w2)
    col2 = Collect(net, at, p2, kv_back, c2_sib, c2_a, c2_b, c2_l, c2_r, c2_f, exchange=False)
    col2.start()
    low = kv_low[...]
    for i in range(4):
        cols = width // 4
        block = tn(lowered[:, i * cols : (i + 1) * cols], low).astype(bf16)
        w_part[i * (cols // kv_part) : (i + 1) * (cols // kv_part)] = block.reshape(cols // kv_part, kv_part, w)
    col2.hop1()

    def index(z, y):
        return lax.rem(z, 2) * CTX + (z // 2) * 4 + y

    order = [lax.rem(at.z + i, 4) for i in (2, 1, 3, 0)]
    rings = []
    for i, z in enumerate(order):
        lands = {"a": w_half.at[i, 0], "b": w_half.at[i, 1], "l": w_whole.at[i, 0], "r": w_whole.at[i, 1]}
        rings.append(RingSum(
            net,
            lambda y, p, z=z: wide(w_part[index(z, y), part_of(p, kv_part)]),
            lambda y, p, i=i: w_stage.at[i, y, part_of(p, kv_part)],
            lambda name, lands=lands: lands[name],
            at.y, at.up, at.down,
        ))
    for ring in rings:
        ring.hop1()
    col2.hop2()
    d_res.hop2()
    for ring in rings:
        ring.hop2()
    col.finish()
    col2.hop3()

    load.wait()
    inputs = wide(toks[...])
    norm = norm_in[0:1, mine]
    gh = grad_hidden[...]
    back = nn(pick_att[...], ret[...].reshape(-1, part))
    back = back[:tok] + back[tok:] + wide(kv_back[...].reshape(tok, part))
    lane = lax.broadcasted_iota(jnp.int32, (tok, 128), 1)
    facts = info[...]
    d0 = jnp.sum(wide(att_picked[:tok, :]) * gh, axis=1, keepdims=True)
    d1 = jnp.sum(wide(att_picked[tok:, :]) * gh, axis=1, keepdims=True)
    inner = jnp.sum(back * norm * inputs, axis=1, keepdims=True)
    sums = jnp.where(lane == 0, d0, jnp.where(lane == 1, d1, jnp.where(lane == 2, inner, 0.0)))
    small_out[...] = to_row_form(sums, 8)
    smalls = [net.go(small_out, small_in.at[j], p) for j, p in enumerate(near_tp)]
    for z, ring in zip(order, rings):
        w_sum[z] = ring.hop3()
    lands = {"a": wz_half.at[0], "b": wz_half.at[1], "l": wz_whole.at[0], "r": wz_whole.at[1]}
    zsum = RingSum(
        net,
        lambda z, p: w_sum[z, part_of(p, kv_part)],
        lambda z, p: wz_stage.at[z, part_of(p, kv_part)],
        lambda name: lands[name],
        at.z, at.above, at.below,
    )
    zsum.hop1()
    total = small_out[...]
    for j, m in enumerate(smalls):
        m.wait_recv()
        total = total + small_in[j]
    sums = to_column_form(total)
    scale, g0, g1 = facts[:, 0:1], facts[:, 1:2], facts[:, 2:3]
    inner = g0 * sums[:, 0:1] + g1 * sums[:, 1:2]
    hot = hot_lanes(routes[...])
    grad_logits = hot[0] * (g0 * (sums[:, 0:1] - inner)) + hot[1] * (g1 * (sums[:, 1:2] - inner))
    grad_low = back
    for e in range(CTX):
        grad_low = grad_low + grad_logits[:, FIRST + e : FIRST + e + 1] * router_t[e : e + 1, mine]
    inner = sums[:, 2:3] + jnp.sum(grad_logits * facts, axis=1, keepdims=True)
    grad = gh + scale * (grad_low * norm) - inputs * (scale * scale * scale) * (inner / width)
    x_in[...] = grad.astype(bf16).reshape(x_in.shape)
    d_in = Dispatch(net, at, x_in, input_grad, exchange=False)
    d_in.start()
    d_in.hop1()
    rgrad[...] = sum(tn(g, lowered[:, mine]) for g in split3(grad_logits))
    norm_grad = jnp.sum(grad_low * inputs * scale, axis=0, keepdims=True)
    row = lax.broadcasted_iota(jnp.int32, (8, part), 0)
    minor[0:8, :] = jnp.where(row == 0, norm_grad, jnp.where(row == 1, norm_mid_grad[0:1, :], 0.0))
    minor[8:16, :] = rgrad[FIRST : FIRST + CTX, :]
    minor[16:24, :] = router_mlp_grad[FIRST : FIRST + CTX, :]
    minors = [net.go(minor, minor_in.at[j], p) for j, p in enumerate(far_all)]
    zsum.hop2()
    moves += bulk(split[1], count)
    d_in.hop2()
    d_res.hop3()
    total = minor[...]
    for j, m in enumerate(minors):
        m.wait_recv()
        total = total + minor_in[j]
    minor_sum[...] = total
    minors = [net.go(minor_sum, minor_out.at[at.t], p) for p in near_tp]
    minor_out[at.t] = total
    d_in.hop3()
    kvw_out[...] = zsum.hop3()
    d_res.finish()
    d_in.finish()
    col2.finish()
    for m in minors + moves:
        m.wait_recv()
    net.drain()


def tail(
    p, dkv, lowered, kv_full, mlp_ret, hidden, gates_mlp, pick_mlp, pick_att, att_picked, grad_hidden, info,
    routes, norm_in, router_t, norm_mid_grad, router_mlp_grad, tokens, bulk, split, cid,
):
    _, _, n, rows, w = p.shape
    _, tok, kw = dkv.shape
    part = kv_full.shape[1]
    n2 = 4
    rows2 = tok // n2
    width = w * TP
    spans = [b[1] for b in bulk]
    land = [VM((tok // 2, kw), bf16)] * 2 + [VM((tok, kw), bf16)] * 2
    col2 = Collect.scratch(n2, rows2, w)
    return pl.pallas_call(
        partial(tail_body, spans, split),
        out_shape=(
            sds((part, kw), f32), sds((tok, width), bf16), sds((tok, width), bf16), sds((TP, 24, w), f32),
        ) + tuple(sds(b[2], b[0].dtype) for b in bulk),
        in_specs=vmem(17) + anywhere(1 + len(bulk)),
        out_specs=tuple(vmem(4) + anywhere(len(bulk))),
        scratch_shapes=Collect.scratch(n, rows, w)
        + [VM((4, tok, kw), bf16)] * 2 + land + land
        + [VM((tok, kw), bf16)] * 3
        + [VM((2, 4, n2, rows2, w), bf16)] + col2
        + [
            VM((FSDP * CTX, part, kw), bf16), VM((4, 4, part, kw), bf16), VM((4, 2, part // 2, kw), bf16),
            VM((4, 2, part, kw), bf16), VM((4, part, kw), f32), VM((4, part, kw), bf16),
            VM((2, part // 2, kw), bf16), VM((2, part, kw), bf16),
            VM((n, 128, w), bf16), VM((n2, rows2, w), bf16), VM((n * 128, w), bf16),
            VM((n2, rows2, w), bf16), VM((n2, rows2, w), bf16), VM((8, tok), f32), VM((TP - 1, 8, tok), f32),
            VM((24, w), f32), VM((FSDP * CTX - 1, 24, w), f32), VM((24, w), f32), VM((128, w), f32),
            VM((tok, w), bf16), DMA((1,)),
        ]
        + sems(Collect.COPIES * 2 + Dispatch.COPIES * 2 + 100),
        compiler_params=params(cid),
        cost_estimate=cost(90),
    )(
        p, dkv, lowered, kv_full, mlp_ret, hidden, gates_mlp, pick_mlp, pick_att, att_picked, grad_hidden, info,
        routes, norm_in, router_t, norm_mid_grad, router_mlp_grad, tokens, *[b[0] for b in bulk],
    )


def mid_body(
    plan,
    p_att, pick_att, pick_mlp, info, routes, norm_mid_full, router_full, tokens, cot, rows_g, gu_own, gu_f, gu_a, down_own,
    att_picked, hidden, gates_out, grad_hidden, norm_grad, router_grad, grad_proj, p1, gu_sent, dd_sent,
    gu_grad, dd_grad, dd_got, gu_got,
    ret, b1_sib, b1_a, b1_b, b1_l, b1_r, fbuf,
    x_slots, X, G, W, D, gun, U, GG, GU, trans, p2, lm, small_out, small_in, small2_out, small2_in,
    sums_ref, gs_out, gs_in, sgm, sg_out, sg_in, sg_tot, sg_home, stage, toks, cots, local_sem, stage_sem, send, recv,
):
    at, net = Place(), Net(send, recv)
    tok, part = lm.shape
    ff = down_own.shape[0]
    half = down_own.shape[1]
    cap = x_slots.shape[1]
    pad = W.shape[1] - ff
    n_f, n_a = gu_f.shape[1], gu_a.shape[1]
    mine = pl.ds(pl.multiple_of(at.f * half, half), half)
    other = pl.ds(pl.multiple_of((1 - at.f) * half, half), half)
    near = tp_peers(at)
    ret[...] = jnp.zeros_like(ret)
    loads = []

    def load(src, dst):
        d = pltpu.make_async_copy(src, dst, local_sem.at[len(loads)])
        d.start()
        loads.append(d)
        return d

    here = pl.ds(pl.multiple_of(at.t * part, part), part)
    load_s = [load(tokens.at[:, here], toks), load(cot.at[:, here], cots)]
    load_g = load(rows_g, G)
    load_d = load(down_own, D.at[pl.ds(0, ff), mine])
    load_w = [
        load(gu_own, W.at[:, pl.ds(0, ff), mine]),
        load(gu_f, W.at[:, pl.ds(0, n_f), other]),
        load(gu_a, W.at[:, pl.ds(n_f, n_a), other]),
    ]
    greet(at.ctx_peers() + near + [at.partner])

    def down_piece(lo, hi):
        s = pl.ds(lo, hi - lo)
        return net.go(down_own.at[s], D.at[s, mine], at.partner)

    d_cut = plan["down"]
    down_moves = [down_piece(0, d_cut[0])]
    W[:, ff:, :] = jnp.zeros_like(W[:, ff:, :])
    D[ff:, :] = jnp.zeros_like(D[ff:, :])
    col1 = Collect(net, at, p_att, ret.at[0], b1_sib, b1_a, b1_b, b1_l, b1_r, fbuf)
    col1.start()
    col1.hop1()
    col1.hop2()
    col1.hop3()
    down_moves.append(down_piece(d_cut[0], d_cut[1]))
    col1.finish()

    lane = lax.broadcasted_iota(jnp.int32, (tok, 128), 1)
    hot = hot_lanes(routes[...])
    ga = [info[:, k : k + 1] for k in (1, 2)]
    norm = norm_mid_full[0:1, here]
    router_t = router_full[:, here]
    router = jnp.concatenate([jnp.zeros((FIRST, part), f32), router_t, jnp.zeros((128 - FIRST - CTX, part), f32)]).T
    for d in load_s:
        d.wait()
    picked = nn(pick_att[...], ret[0].reshape(-1, part))
    att_picked[...] = picked.astype(bf16)
    h = wide(toks[...]) + ga[0] * picked[:tok] + ga[1] * picked[tok:]
    hidden[...] = h
    raw = exact(h * norm, router)
    sums = jnp.where(lane == 0, jnp.sum(h * h, axis=1, keepdims=True), raw)
    small_out[...] = to_row_form(sums, 16)
    moves = [net.go(small_out, small_in.at[j], p) for j, p in enumerate(near)]
    total = small_out[...]
    for j, m in enumerate(moves):
        m.wait_recv()
        total = total + small_in[j]
    sums = to_column_form(total)
    scale = lax.rsqrt(sums[:, 0:1] / (part * TP) + epsilon)
    low = [jnp.sum(o * sums, axis=1, keepdims=True) * scale for o in hot]
    g0 = 1.0 / (1.0 + jnp.exp(low[1] - low[0]))
    g1 = 1.0 / (1.0 + jnp.exp(low[0] - low[1]))
    gates = jnp.where(lane == 0, g0, jnp.where(lane == 1, g1, jnp.where(lane == 2, scale, 0.0)))
    sums_ref[...] = sums
    gates_out[...] = gates
    lm[...] = (hidden[...] * scale * norm).astype(bf16)
    slots = tn(pick_mlp[:tok, :] + pick_mlp[tok:, :], lm[...]).astype(bf16)
    for e in range(CTX):
        x_slots[e] = slots[e * 128 : e * 128 + cap]
    d1 = Dispatch(net, at, x_slots, X)
    d1.start()
    rows2 = to_row_form(gates, 2)
    pair_row = jnp.concatenate([rows2[0:1], rows2[1:2]], axis=1)
    slot_gates = jnp.sum(nn(three_rows(pair_row), pick_mlp[...]), axis=0, keepdims=True)
    for e in range(CTX):
        gs_out[e] = jnp.broadcast_to(slot_gates[:, e * 128 : (e + 1) * 128], (8, 128))
    gs_moves = [net.go(gs_out.at[p["ctx"]], gs_in.at[at.c], p) for p in at.ctx_peers()]
    gs_in[at.c] = gs_out[at.c]
    down_moves.append(down_piece(d_cut[1], ff))
    last = pl.ds(n_f + n_a, ff - n_f - n_a)
    gu_move = net.go(gu_own.at[:, last], W.at[:, last, mine], at.partner)
    d1.hop1()
    for m in gs_moves:
        m.wait_recv()
    load_g.wait()
    for b in range(CTX):
        column = gs_in[b].T[:cap, 0:1]
        s = slice(b * cap, (b + 1) * cap)
        G[s, :] = (wide(G[s, :]) * column).astype(bf16)
    d1.hop2()
    load_d.wait()
    for m in down_moves:
        m.wait_recv()
    rows_at = 2 * cap
    groups = CTX // 2

    def group_rows(g):
        return pl.ds(pl.multiple_of(g * rows_at, rows_at), rows_at)

    @pl.loop(0, groups)
    def _(g):
        s = group_rows(g)
        gun[s, :] = nt(G[s, :], D[...])

    d1.hop3()
    d1.finish()
    for m in load_w:
        m.wait()
    gu_move.wait_recv()
    sgm[...] = jnp.zeros_like(sgm)

    def put(p_ref, g, out):
        for i in range(TP):
            for b in range(2):
                p_ref[i % 2, i // 2, 2 * g + b] = out[b * cap : (b + 1) * cap, i * part : (i + 1) * part]

    @pl.loop(0, groups)
    def _(g):
        s = group_rows(g)
        x = X[s, :]
        gate = nt(x, W[0])
        up = nt(x, W[1])
        sig = 1.0 / (1.0 + jnp.exp(-gate))
        silu = gate * sig
        units = (silu * up).astype(bf16)
        grad = gun[s, :]
        d_gate = (grad * up * (sig * (1.0 + gate * (1.0 - sig)))).astype(bf16)
        d_up = (grad * silu).astype(bf16)
        U[s, :] = units
        GG[s, :] = d_gate
        GU[s, :] = d_up
        column = jnp.sum(wide(units) * grad, axis=1, keepdims=True)
        for b in range(2):
            sgm[2 * g + b, :cap, :] = jnp.broadcast_to(column[b * cap : (b + 1) * cap], (cap, 128))
        put(p2, g, (nn(d_gate, W[0]) + nn(d_up, W[1])).astype(bf16))

    col2 = Collect(net, at, p2, ret.at[1], b1_sib, b1_a, b1_b, b1_l, b1_r, fbuf)
    net.drain()
    col2.start()
    for b in range(CTX):
        sg_out[b] = sgm[b].T[:8]
    sg_moves = [net.go(sg_out, sg_in.at[j], p) for j, p in enumerate(near)]

    @pl.loop(0, groups)
    def _(g):
        s = group_rows(g)
        put(p1, g, nn(U[s, :], D[...]).astype(bf16))

    col2.hop1()
    v = sg_out[...]
    for j, m in enumerate(sg_moves):
        m.wait_recv()
        v = v + sg_in[j]
    sg_tot[...] = v
    sg_moves = [net.go(sg_tot.at[p["ctx"]], sg_home.at[at.c], p) for p in at.ctx_peers()]
    sg_home[at.c] = sg_tot[at.c]

    cols = stage.shape[2]
    steps = half // cols
    trans[...] = U[...].T

    @pl.loop(0, steps)
    def _(i):
        src = pl.ds(pl.multiple_of((1 - at.f) * half + i * cols, cols), cols)
        dd_sent[:, pl.ds(pl.multiple_of(i * cols, cols), cols)] = nn(trans[...], G[:, src])[:ff].astype(bf16)

    cut = plan["dd"]
    got_moves = []

    def dd_piece(lo, hi):
        s = pl.ds(lo, hi - lo)
        got_moves.append(net.go(dd_sent.at[s], dd_got.at[s], at.partner))

    dd_piece(0, cut[0])
    col2.hop2()

    def own_part(matrix, dst, first):
        out = []
        for i in range(steps):
            slot = (first + i) % 2
            if first + i >= 2:
                stage_copies[first + i - 2].wait()
            src = pl.ds(pl.multiple_of(at.f * half + i * cols, cols), cols)
            stage[slot] = nn(trans[...], matrix[:, src])[:ff]
            d = pltpu.make_async_copy(stage.at[slot], dst(pl.ds(i * cols, cols)), stage_sem.at[slot])
            d.start()
            stage_copies.append(d)

    stage_copies = []
    own_part(G, lambda s: dd_grad.at[:, s], 0)
    col2.hop3()
    dd_piece(cut[0], cut[1])
    for j, grads in enumerate((GG, GU)):
        trans[...] = grads[...].T

        @pl.loop(0, steps)
        def _(i):
            src = pl.ds(pl.multiple_of((1 - at.f) * half + i * cols, cols), cols)
            gu_sent[j, :, pl.ds(pl.multiple_of(i * cols, cols), cols)] = nn(trans[...], X[:, src])[:ff].astype(bf16)

        if j == 0:
            own_part(X, lambda s: gu_grad.at[0, :, s], steps)
    col2.finish()

    lane = lax.broadcasted_iota(jnp.int32, (tok, 128), 1)
    hot = hot_lanes(routes[...])
    ga = [info[:, k : k + 1] for k in (1, 2)]
    norm = norm_mid_full[0:1, here]
    router_t = router_full[:, here]
    sums = sums_ref[...]
    gates = gates_out[...]
    scale = gates[:, 2:3]
    back = nn(pick_mlp[...], ret[1].reshape(-1, part))
    back = back[:tok] + back[tok:]
    h = hidden[...]
    inner = jnp.sum(back * norm * h, axis=1, keepdims=True)
    small2_out[...] = to_row_form(jnp.where(lane == 0, inner, 0.0), 8)
    moves = [net.go(small2_out, small2_in.at[j], p) for j, p in enumerate(near)]
    for m in sg_moves:
        m.wait_recv()
    row = jnp.concatenate([sg_home[e][0:1] for e in range(CTX)], axis=1)
    pairs = jnp.sum(nt(pick_mlp[...], three_rows(row)), axis=1, keepdims=True)
    sg = [pairs[:tok], pairs[tok:]]
    grad_logits = sum(
        o * (d - gates[:, k : k + 1] * (sg[0] + sg[1])) for k, (o, d) in enumerate(zip(hot, sg))
    )
    grad_low = back
    for e in range(CTX):
        grad_low = grad_low + grad_logits[:, FIRST + e : FIRST + e + 1] * router_t[e : e + 1, :]
    total = small2_out[...]
    for j, m in enumerate(moves):
        m.wait_recv()
        total = total + small2_in[j]
    inner = to_column_form(total)[:, 0:1] + jnp.sum(grad_logits * sums, axis=1, keepdims=True)
    gh = (
        wide(cots[...]) + scale * (grad_low * norm) - h * (scale * scale * scale) * (inner / (part * TP))
    )
    grad_hidden[...] = gh
    pair_rows = jnp.concatenate([(ga[0] * gh).astype(bf16), (ga[1] * gh).astype(bf16)], axis=0)
    slots = tn(pick_att[...], pair_rows).astype(bf16)
    for e in range(CTX):
        x_slots[e] = slots[e * 128 : e * 128 + cap]
    d2 = Dispatch(net, at, x_slots, grad_proj)
    d2.start()
    dd_piece(cut[1], ff)
    rows = gu_got.shape[1]
    got_moves.append(net.go(gu_sent.at[:, pl.ds(0, rows)], gu_got, at.partner))
    norm_grad[...] = jnp.broadcast_to(jnp.sum(grad_low * h * scale, axis=0, keepdims=True), norm_grad.shape)
    router_grad[...] = sum(tn(g, lm[...]) for g in split3(grad_logits))
    d2.hop1()
    d2.hop2()
    own_part(X, lambda s: gu_grad.at[1, :, s], 2 * steps)
    d2.hop3()
    d2.finish()
    for d in stage_copies[-2:]:
        d.wait()
    for m in got_moves:
        m.wait_recv()
    net.drain()


def mid(
    plan, p_att, pick_att, pick_mlp, info, routes, norm_mid, router_t, tokens, cot, rows_g, gu_own, gu_f, gu_a, down_own, cid,
):
    tok, width = tokens.shape
    part = width // TP
    _, _, n, cap, _ = p_att.shape
    slots, width = rows_g.shape
    ff, half = down_own.shape
    ffp = (ff + 255) // 256 * 256
    cols = 256
    bufs = Collect.scratch(n, cap, part)
    vm_out = (
        sds((2 * tok, part), bf16), sds((tok, part), f32), sds((tok, 128), f32), sds((tok, part), f32),
        sds((8, part), f32), sds((128, part), f32), sds((slots, width), bf16), sds(p_att.shape, bf16),
        sds((2, ff, half), bf16), sds((ff, half), bf16),
    )
    any_out = (sds((2, ff, half), f32), sds((ff, half), f32), sds((ff, half), bf16), sds((2, plan["gu"], half), bf16))
    return pl.pallas_call(
        partial(mid_body, plan),
        out_shape=vm_out + any_out,
        in_specs=vmem(7) + anywhere(7),
        out_specs=tuple(vmem(len(vm_out)) + anywhere(len(any_out))),
        scratch_shapes=[VM((2, n, 128, part), bf16)] + bufs
        + [
            VM((n, cap, part), bf16), VM((slots, width), bf16), VM((slots, width), bf16),
            VM((2, ffp, width), bf16), VM((ffp, width), bf16), VM((slots, ffp), f32),
            VM((slots, ffp), bf16), VM((slots, ffp), bf16), VM((slots, ffp), bf16), VM((ffp, slots), bf16),
            VM(p_att.shape, bf16), VM((tok, part), bf16),
            VM((16, tok), f32), VM((TP - 1, 16, tok), f32), VM((8, tok), f32), VM((TP - 1, 8, tok), f32),
            VM((tok, 128), f32), VM((n, 8, 128), f32), VM((n, 8, 128), f32), VM((n, 128, 128), f32),
            VM((n, 8, 128), f32), VM((TP - 1, n, 8, 128), f32), VM((n, 8, 128), f32), VM((n, 8, 128), f32),
            VM((2, ff, cols), f32), VM((tok, part), bf16), VM((tok, part), bf16), DMA((8,)), DMA((2,)),
        ]
        + sems(2 * Collect.COPIES + 2 * Dispatch.COPIES + 64),
        compiler_params=params(cid),
        cost_estimate=cost(140),
    )(
        p_att, pick_att, pick_mlp, info, routes, norm_mid, router_t, tokens, cot, rows_g, gu_own, gu_f, gu_a, down_own,
    )


def attend_back_body(
    cap, tok, span,
    grad_proj, rows_ref, q_ref, kv_ref, pos_ref, att_ref, lse_ref, p1, q_own, q_oth, o_own, o_oth, bulk_ref,
    dkv_ref, p3, mlp_ret, o_grad, q_grad, o_sent, q_sent, bulk_out,
    wq, wo, do_ref, dq_ref, kt_ref, acc_ref, b_sib, b_a, b_b, b_l, b_r, fbuf, local_sem, send, recv,
):
    at, net = Place(), Net(send, recv)
    heads = q_ref.shape[1] // HD
    width = heads * HD
    scale = HD ** (-0.5)
    total = q_ref.shape[0]
    load_o = assemble(o_own, o_oth, wo, 1, at.f, local_sem.at[0])
    load_q = assemble(q_own, q_oth, wq, 0, at.f, local_sem.at[1])
    greet(at.ctx_peers() + at.tp_near() + [at.partner])
    lo, size = span
    move = net.go(bulk_ref.at[:, pl.ds(lo, size)], bulk_out, at.partner)
    col = Collect(net, at, p1, mlp_ret, b_sib, b_a, b_b, b_l, b_r, fbuf)
    col.start()
    for h in range(heads):
        kt_ref[h] = kv_ref[:, h * HD : (h + 1) * HD].T
    for d in load_o:
        d.wait()
    do_ref[...] = nt(grad_proj[...], wo[...]).astype(bf16)
    col.hop1()
    acc_ref[...] = jnp.zeros_like(acc_ref)
    rows_at, keys_at = 2 * cap, 2 * tok
    for d in load_q:
        d.wait()
    groups = total // rows_at
    for step, g in enumerate(reversed(range(groups))):
        lo = g * rows_at
        rows = slice(lo, lo + rows_at)
        extent = (g + 1) * keys_at
        at_key = extent - keys_at
        pos = pair_positions(pos_ref, g, cap)
        for h in range(heads):
            cols = slice(h * HD, (h + 1) * HD)
            vcols = slice(width + h * HD, width + (h + 1) * HD)
            q = q_ref[rows, cols]
            do = do_ref[rows, cols]
            s = nt(kv_ref[:extent, cols], q) * scale
            lse = lse_ref[h : h + 1, rows]
            ids = lax.broadcasted_iota(jnp.int32, (keys_at, rows_at), 0) + at_key
            last = jnp.where(ids <= pos, s[at_key:], masked_score)
            s = jnp.concatenate([s[:at_key], last], axis=0) if g else last
            soft = jnp.exp(s - lse)
            dp = nt(kv_ref[:extent, vcols], do)
            inner = jnp.sum(soft * dp, axis=0, keepdims=True)
            ds = (soft * (dp - inner)).astype(bf16)
            acc_ref[:extent, vcols] += nn(soft.astype(bf16), do)
            acc_ref[:extent, cols] += nn(ds, q)
            dq_ref[rows, cols] = (nn(kt_ref[h, :, :extent], ds) * scale).T.astype(bf16)
        out = nt(dq_ref[rows, :], wq[...]).astype(bf16)
        for i in range(TP):
            for b in range(2):
                p3[i % 2, i // 2, 2 * g + b] = out[b * cap : (b + 1) * cap, i * width : (i + 1) * width]
        if step == 0:
            col.hop2()
        if step == 1:
            col.hop3()
    dkv_ref[:, :width] = (acc_ref[:, :width] * scale).astype(bf16)
    dkv_ref[:, width:] = acc_ref[:, width:].astype(bf16)
    half = o_own.shape[1]
    step_cols = 256
    att_t = att_ref[...].T
    for i in range(half // step_cols):
        here = slice(i * step_cols, (i + 1) * step_cols)
        mine = pl.ds(pl.multiple_of(at.f * half + i * step_cols, step_cols), step_cols)
        other = pl.ds(pl.multiple_of((1 - at.f) * half + i * step_cols, step_cols), step_cols)
        o_sent[:, here] = nn(att_t, grad_proj[:, other]).astype(bf16)
        o_grad[:, here] = nn(att_t, grad_proj[:, mine])
        q_sent[here, :] = tn(rows_ref[:, other], dq_ref[...]).astype(bf16)
        q_grad[here, :] = tn(rows_ref[:, mine], dq_ref[...])
    col.finish()
    move.wait_recv()
    net.drain()


def attend_back(grad_proj, rows_att, q, kv, pos, att, lse, p1, q_own, q_oth, o_own, o_oth, bulk, span, tok, cap, cid):
    heads = q.shape[1] // HD
    slots, width = rows_att.shape
    w = heads * HD
    half = width // 2
    _, _, n, _, part = p1.shape
    return pl.pallas_call(
        partial(attend_back_body, cap, tok, span),
        out_shape=(
            sds(kv.shape, bf16), sds(p1.shape, bf16), sds((n, cap, part), bf16), sds((w, half), f32),
            sds((half, w), f32), sds((w, half), bf16), sds((half, w), bf16), sds((2, span[1], bulk.shape[2]), bf16),
        ),
        in_specs=vmem(8) + anywhere(5),
        out_specs=tuple(vmem(7) + anywhere(1)),
        scratch_shapes=[
            VM((width, w), bf16), VM((w, width), bf16), VM((slots, w), bf16), VM((slots, w), bf16),
            VM((heads, HD, kv.shape[0]), bf16), VM(kv.shape, f32),
        ]
        + Collect.scratch(n, cap, part) + [DMA((2, 2))] + sems(Collect.COPIES + 1),
        compiler_params=params(cid),
        cost_estimate=cost(35),
    )(grad_proj, rows_att, q, kv, pos, att, lse, p1, q_own, q_oth, o_own, o_oth, bulk)


def local(
    tokens, norm_in, norm_mid, router_att, router_mlp, kv_weight, query_weight, output_weight,
    gate_up_weight, down_weight, routes_att, routes_mlp, cotangent,
):
    f, c = lax.axis_index("fsdp"), lax.axis_index("ctx")
    count_rows, width = tokens.shape[1:]
    capacity = count_rows * 2 // CTX
    half = width // 2
    local_width = query_weight.shape[2]
    tokens, cotangent = tokens[0], cotangent[0]
    q_own, o_own, down_own = query_weight[0], output_weight[0], down_weight[0]
    gu_own = gate_up_weight[0].transpose(0, 2, 1)
    routes_att, routes_mlp = routes_att[0].T, routes_mlp[0].T
    norm_in, norm_mid = norm_in[None], norm_mid[None]
    router_att, router_mlp = router_att.T, router_mlp.T
    hidden_count = gu_own.shape[1]
    unit = hidden_count // 44
    gu_front, gu_attend = 8 * unit, 16 * unit
    plan = {"down": (22 * unit, 36 * unit), "dd": (10 * unit, 22 * unit), "gu": 4 * unit}
    gu_back, gu_tail = 24 * unit, 14 * unit

    rows_att, rows_g, kv_seq, kv_full, positions, lowered, pick_att, pick_mlp, info, q_oth, o_oth, gu_0 = front(
        tokens, norm_in, router_att, routes_att, routes_mlp, cotangent, kv_weight, q_own, o_own, gu_own,
        capacity, gu_front, 1,
    )
    kv_seq = kv_seq.reshape(-1, 2 * local_width)
    queries, attended, log_totals, p_att, gu_1 = attend(
        rows_att, q_own, q_oth, o_own, o_oth, kv_seq, positions, gu_own, count_rows, capacity, gu_front, gu_attend, 2
    )
    (
        att_picked, hidden, gates_mlp, grad_hidden, norm_mid_grad, router_mlp_grad, grad_proj, p_mlp, gu_sent, dd_sent,
        gu_grad, dd_grad, dd_got, gu_got_0,
    ) = mid(
        plan, p_att, pick_att, pick_mlp, info, routes_mlp, norm_mid, router_mlp, tokens, cotangent,
        rows_g, gu_own, gu_0, gu_1, down_own, 3,
    )
    dkv, p_back, mlp_ret, o_grad, q_grad, o_sent, q_sent, gu_got_1 = attend_back(
        grad_proj, rows_att, queries, kv_seq, positions, attended, log_totals, p_mlp, q_own, q_oth, o_own, o_oth,
        gu_sent, (plan["gu"], gu_back), count_rows, capacity, 4,
    )
    at_tail = plan["gu"] + gu_back
    last = hidden_count - at_tail - gu_tail
    bulk = [
        (gu_sent, lambda r: r.at[:, pl.ds(at_tail, gu_tail)], (2, gu_tail, half)),
        (gu_sent, lambda r: r.at[:, pl.ds(at_tail + gu_tail, last)], (2, last, half)),
        (o_sent, lambda r: r, o_sent.shape),
        (q_sent, lambda r: r, q_sent.shape),
    ]
    kvw_grad, result, input_grad, minor, gu_got_2, gu_got_3, o_got, q_got = tail(
        p_back, dkv.reshape(CTX, count_rows, 2 * local_width), lowered, kv_full, mlp_ret, hidden, gates_mlp,
        pick_mlp, pick_att, att_picked, grad_hidden, info, routes_att, norm_in, router_att,
        norm_mid_grad, router_mlp_grad, tokens, bulk, (1, 3), 5,
    )
    me = f * CTX + c
    minor = lax.dynamic_index_in_dim(minor, me // 2, 0, keepdims=False)
    minor = lax.dynamic_slice_in_dim(minor, lax.rem(me, 2) * 128, 128, 1)
    gu_got = jnp.concatenate([gu_got_0, gu_got_1, gu_got_2, gu_got_3], axis=1)
    gate_up_grad = gu_grad + gu_got.astype(f32)
    return (
        result[None], input_grad.astype(f32)[None], minor[0], minor[1], minor[8:16].T, minor[16:24].T,
        jnp.stack([kvw_grad[:, :local_width], kvw_grad[:, local_width:]]),
        (q_grad + q_got.astype(f32))[None], (o_grad + o_got.astype(f32))[None],
        gate_up_grad.transpose(0, 2, 1)[None], (dd_grad + dd_got.astype(f32))[None],
    )


def solution(mesh):
    placed = (
        P("fsdp", "ctx", None), P(), P(), P(), P(),
        P(None, ("fsdp", "ctx"), "tp"), P("ctx", "fsdp", "tp"), P("ctx", "tp", "fsdp"),
        P("ctx", None, "fsdp", "tp"), P("ctx", "tp", "fsdp"),
        P("fsdp", "ctx", None), P("fsdp", "ctx", None), P("fsdp", "ctx", None),
    )
    return jax.shard_map(
        local,
        mesh=mesh,
        in_specs=placed,
        out_specs=(
            P("fsdp", "ctx", None), P("fsdp", "ctx", None), P(("fsdp", "ctx")), P(("fsdp", "ctx")),
            P(("fsdp", "ctx"), None), P(("fsdp", "ctx"), None), P(None, ("fsdp", "ctx"), "tp"),
            P("ctx", "fsdp", "tp"), P("ctx", "tp", "fsdp"), P("ctx", None, "fsdp", "tp"), P("ctx", "tp", "fsdp"),
        ),
        check_vma=False,
    )
```

time: 1650 us -> 451 us (0.27)
  waiting for transfers between devices: 477 us -> 0 us
  Pallas kernels: 0 us -> 422 us
  blocking collectives: 412 us -> 0 us
  local copies, waits for them, and re-layouts: 306 us -> 4.53 us
  other arithmetic: 214 us -> 14.7 us
  matrix products: 156 us -> 0 us
  starting transfers between devices: 50 us -> 0 us
    pallas_call x0 -> x5, Pallas kernels: none -> 422 us  [the longest x1 172 us: mid(): pl.pallas_call(partial(mid_body, plan), out_shape=vm_out + any_out, in_sp...]
    psum x3 -> x0, blocking collectives: 306 us -> none  [to_home(): summed = lax.psum(partial_rows, 'tp')]
    reduce_scatter x4 -> x0, waiting for transfers between devices: 168 us -> none  [the longest x1 78.9 us: local(): lax.psum_scatter(down_grad.astype(jnp.bfloat16), 'fsdp', scatter_dimensio...]
    dot_general x27 -> x0, matrix products: 156 us -> none  [the longest x1 12.3 us: attend_backward(): jnp.einsum('rhk,shk->hrs', grad_block, values_heads, preferred_element_ty...]
    unnamed x165 -> x19, local copies, waits for them, and re-layouts: 128 us -> 1.77 us
    all_gather x6 -> x0, waiting for transfers between devices: 98.9 us -> none  [the longest x1 61.9 us: local(): kv_full = lax.all_gather(kv_weight, ('fsdp', 'ctx'), axis=1, tiled=True)]
    all_to_all x7 -> x0, waiting for transfers between devices: 84.2 us -> none  [the longest x4 68.4 us: to_experts(): lax.all_to_all(home_rows, 'ctx', split_axis=0, concat_axis=0, tiled=True)]
    reduce_sum x17 -> x0, other arithmetic: 68.3 us -> none  [the longest x4 45.8 us: combine_rows(): return (jnp.sum(picked * weight[:, :, None], axis=1), picked)]
  transfers between devices with their start and end apart: 22 -> 0, of which waited for: 13 -> 0; matrix products, arithmetic and copies ran while one was open for 33% -> 0% of each run, Pallas kernels for 0% -> 0%
where the time goes in v1:
time: 451 us; the launch traced here: 442 us
  Pallas kernels  422 us (94%)
  other arithmetic  14.7 us (3%)
  local copies, waits for them, and re-layouts  4.53 us (1%)
    pallas_call x1, Pallas kernels, mid(): pl.pallas_call(partial(mid_body, plan), out_shape=vm_out + any_out, in_sp...  172 us
    pallas_call x1, Pallas kernels, tail(): pl.pallas_call(partial(tail_body, spans, split), out_shape=(sds((part, kw...  98.6 us
    pallas_call x1, Pallas kernels, front(): pl.pallas_call(front_body, out_shape=(wide_rows, wide_rows, sds((CTX, tok...  80.8 us
    pallas_call x1, Pallas kernels, attend_back(): pl.pallas_call(partial(attend_back_body, cap, tok, span), out_shape=(sds(...  51.3 us
    pallas_call x1, Pallas kernels, attend(): pl.pallas_call(partial(attend_body, cap, tok, first), out_shape=(sds((slo...  19.5 us

profile of v1, /device:TPU:1, one launch (start us, length us, event | category | flops | bytes accessed | tf_op | source)
XLA Modules:
  0.0 442.2 jit_solution(3111826680409344530)
XLA Ops:
  0.6 80.8 %shard_map.212 = (bf16[768,2048]{1,0:T(8,128)(2,1)}, bf16[768,2048]{1,0:T(8,128)(2,1)}, bf16[8,384,512]{2,1,0:T(8,128)(2,1)}, bf16[16,128,512]{2,1,0:T(8,128)(2,...) custom-call(bf16[384,2048]{1,0:T(8,128)(2,1)} %bitcast.53, ...), custom_call_target="tpu_custom_call" | custom-call | bytes 224000000 | tf_op jit(solution)/shard_map/pallas_call | solution.py:487
  81.4 19.5 %shard_map.213 = (bf16[768,256]{1,0:T(8,128)(2,1)}, bf16[768,256]{1,0:T(8,128)(2,1)}, f32[2,768]{1,0:T(2,128)}, bf16[2,4,8,96,256]{4,3,2,1,0:T(8,128)(2,1)}, bf16[2,256,1024]{2,1,0:T(8,128)(2,1)}) custom-call(bf16[768,2048]{1,0:T(8,128)(2,1)} %get-tuple-element.57.rows_ref, bf16[1024,256]{1,0:T(8,128)(2,1)} %bitcast.61, ...), custom_call_target="tpu_custom_call" | custom-call | bytes 80000000 | tf_op jit(solution)/shard_map/pallas_call | solution.py:572
  101.0 171.8 %shard_map.214 = (bf16[768,256]{1,0:T(8,128)(2,1)}, f32[384,256]{1,0:T(8,128)}, f32[384,128]{1,0:T(8,128)}, f32[384,256]{1,0:T(8,128)}, f32[8,256]{1,0:T(8,128)}...) custom-call(bf16[2,4,8,96,256]{4,3,2,1,0:T(8,128)(2,1)} %get-tuple-e, ...), custom_call_target="tpu_custom_call" | custom-call | bytes 448000000 | tf_op jit(solution)/shard_map/pallas_call | solution.py:1116
  272.8 4.5 %add_bitcast_fusion.1 = f32[1,704,1024]{2,1,0:T(8,128)} fusion(f32[704,1024]{1,0:T(8,128)} %get-tuple-element.101, bf16[704,1024]{1,0:T(8,128)(2,1)} %get-tuple-element.102), kind=kLoop, calls=%fused_computation.1 | loop fusion | flops 1441792 | bytes 7208960 | tf_op jit(solution)/shard_map/broadcast_in_dim | solution.py:1304
  277.2 51.3 %shard_map.215 = (bf16[3072,512]{1,0:T(8,128)(2,1)}, bf16[2,4,8,96,256]{4,3,2,1,0:T(8,128)(2,1)}, bf16[8,96,256]{2,1,0:T(8,128)(2,1)}, f32[256,1024]{1,0:T(8,128...) custom-call(bf16[768,2048]{1,0:T(8,128)(2,1)} %get-tuple-element.69., ...), custom_call_target="tpu_custom_call" | custom-call | bytes 112000000 | tf_op jit(solution)/shard_map/pallas_call | solution.py:1224
  328.6 0.0 copy-start
  328.6 0.0 copy-start.7
  328.6 98.6 %shard_map.216 = (f32[128,512]{1,0:T(8,128)}, bf16[384,2048]{1,0:T(8,128)(2,1)}, bf16[384,2048]{1,0:T(8,128)(2,1)}, f32[8,24,256]{2,1,0:T(8,128)}, bf16[2,224,10...) custom-call(bf16[2,4,8,96,256]{4,3,2,1,0:T(8,128)(2,1)} %get-tuple-eleme, ...), custom_call_target="tpu_custom_call" | custom-call | bytes 288000000 | tf_op jit(solution)/shard_map/pallas_call | solution.py:791
  427.3 0.0 copy-done
  427.3 0.0 copy-done.7
  427.3 0.0 copy-start.4
  427.3 0.0 copy-start.6
  427.3 5.3 %add_bitcast_fusion = f32[1,2,1024,704]{2,3,1,0:T(8,128)} fusion(f32[2,704,1024]{2,1,0:T(8,128)} %get-tuple-element.96, bf16[2,32,1024]{2,1,0:T(8,128)(2,1)} %get-tuple-element.100, bf16[2,224,1024]{2,1,0:T(8,128)(2,1)} %get-tuple-element.99, bf16[2,384,1024]{2,1,0:T(8,128)(2,1)S(1)} %copy-done, bf16[2,64,1024]{2,1,0:T(8,128)(2,1)S(1)} %copy-done.7), kind=kLoop, calls=%fused_computation | loop fusion | flops 12976128 | bytes 14417920 | tf_op jit(solution)/shard_map/broadcast_in_dim | solution.py:1304
  432.6 0.0 copy-start.3
  432.6 0.0 copy-start.5
  432.6 0.0 copy-start.8
  432.6 0.0 copy-done.4
  432.6 0.0 copy-done.6
  432.6 0.0 copy-start.2
  432.6 1.1 add_bitcast_fusion.2
  433.7 0.4 copy-done.3
  434.1 0.2 copy-done.5
  434.3 1.1 add_bitcast_fusion.3
  435.4 0.0 copy-done.8
  435.4 0.0 copy-start.1
  435.4 0.7 pad_maximum_fusion
  436.1 0.0 copy-done.2
  436.1 2.0 bitcast_convert_fusion
  438.2 1.4 dynamic-slice_bitcast_fusion
  439.6 1.4 dynamic-slice_bitcast_fusion.2
  440.9 0.0 copy-done.1
  440.9 1.1 copy.25
  (1 shorter events, 0.0 us)
Async XLA Ops:
  328.6 98.7 %copy-start = (bf16[2,384,1024]{2,1,0:T(8,128)(2,1)S(1)}, bf16[2,384,1024]{2,1,0:T(8,128)(2,1)}, u32[]{:S(2)}) copy-start(bf16[2,384,1024]{2,1,0:T(8,128)(2,1)} %get-tuple-element.98) | copy-start | bytes 4718596
  328.6 98.7 %copy-start.7 = (bf16[2,64,1024]{2,1,0:T(8,128)(2,1)S(1)}, bf16[2,64,1024]{2,1,0:T(8,128)(2,1)}, u32[]{:S(2)}) copy-start(bf16[2,64,1024]{2,1,0:T(8,128)(2,1)} %get-tuple-element.97) | copy-start | bytes 786436
  427.3 5.3 %copy-start.4 = (f32[256,1024]{1,0:T(8,128)S(1)}, f32[256,1024]{1,0:T(8,128)}, u32[]{:S(2)}) copy-start(f32[256,1024]{1,0:T(8,128)} %get-tuple-element.94) | copy-start | bytes 3145732
  427.3 5.3 %copy-start.6 = (bf16[256,1024]{1,0:T(8,128)(2,1)S(1)}, bf16[256,1024]{1,0:T(8,128)(2,1)}, u32[]{:S(2)}) copy-start(bf16[256,1024]{1,0:T(8,128)(2,1)} %get-tuple-element.95) | copy-start | bytes 1572868
  432.6 1.5 copy-start.3
  432.6 1.7 copy-start.5
  432.6 2.8 copy-start.8
  432.6 3.5 copy-start.2
  435.4 5.5 %copy-start.1 = (bf16[384,2048]{1,0:T(8,128)(2,1)S(1)}, bf16[384,2048]{1,0:T(8,128)(2,1)}, u32[]{:S(2)}) copy-start(bf16[384,2048]{1,0:T(8,128)(2,1)} %get-tuple-element.88) | copy-start | bytes 4718596
